TPU v7x, 256 devices: a whole 4x4x8 slice. The times are simulated.
256 devices in a mesh: ia: 8 (over z), ja: 16 (over x, y_lo, core), ka: 2 (over y_hi).
Axes of the slice: x: 4, y: 4 (y_hi: 2, y_lo: 2; y = y_hi * 2 + y_lo), z: 8, core: 2. Of those that a mesh axis runs over, the one named last changes fastest.
Arguments:
- tensor: float32 [1024, 1024, 512], P('ia', 'ja', 'ka'), may hold values from -6 to 6
- factor_b: float32 [16, 64, 256], P('ja', ('ia', 'ka')), may hold values from -0.1875 to 0.1875
- factor_c: float32 [2, 256, 256], P('ka', ('ia', 'ja')), may hold values from -0.25 to 0.25
Outputs:
- new_a: float32 [8, 128, 256], P('ia', ('ja', 'ka'))
- new_b: float32 [16, 64, 256], P('ja', ('ia', 'ka'))
- new_c: float32 [2, 256, 256], P('ka', ('ia', 'ja'))
All inputs are finite; a program needn't handle non-finite values.
Results may differ from a plain program's by a relative error of at most 0.00011.
Values sent between devices are 32-bit elements; how exact they have to be, the bound alone decides.
A program may use at most 64 MiB of HBM per device.

v0:
```python
import jax
import jax.numpy as jnp
from jax import lax
from jax.sharding import PartitionSpec as P

HIGH = lax.Precision.HIGHEST


def gram_of(rows):
    return jnp.dot(rows.T, rows, precision=HIGH, preferred_element_type=jnp.float32)


def solve_rows(right, gram):
    factor = jnp.linalg.cholesky(gram)
    return jax.scipy.linalg.cho_solve((factor, True), right.T).T


def on_device(tensor, factor_b, factor_c):
    i_dev, j_dev, k_dev = tensor.shape
    b_slice = lax.all_gather(factor_b, ("ia", "ka"), axis=1, tiled=True)[0]
    c_slice = lax.all_gather(factor_c, ("ia", "ja"), axis=1, tiled=True)[0]
    gram_b, gram_c = lax.psum((gram_of(factor_b[0]), gram_of(factor_c[0])), ("ia", "ja", "ka"))
    partial_t = jnp.einsum("ijk,kr->ijr", tensor, c_slice, precision=HIGH)
    partial_a = jnp.einsum("ijr,jr->ir", partial_t, b_slice, precision=HIGH)
    mttkrp_a = lax.psum_scatter(partial_a, ("ja", "ka"), scatter_dimension=0, tiled=True)
    new_a = solve_rows(mttkrp_a, gram_b * gram_c)
    a_slice = lax.all_gather(new_a[None], ("ja", "ka"), axis=1, tiled=True)[0]
    gram_a = lax.psum(gram_of(new_a), ("ia", "ja", "ka"))
    inner = jnp.einsum("ijk,ir->jkr", tensor, a_slice, precision=HIGH)
    partial_b = jnp.einsum("jkr,kr->jr", inner, c_slice, precision=HIGH)
    mttkrp_b = lax.psum_scatter(partial_b, ("ia", "ka"), scatter_dimension=0, tiled=True)
    new_b = solve_rows(mttkrp_b, gram_a * gram_c)
    b_new_slice = lax.all_gather(new_b[None], ("ia", "ka"), axis=1, tiled=True)[0]
    gram_b_new = lax.psum(gram_of(new_b), ("ia", "ja", "ka"))
    weights = (a_slice[:, None, :] * b_new_slice[None, :, :]).reshape(i_dev * j_dev, -1)
    flat = tensor.reshape(i_dev * j_dev, k_dev)
    partial_c = jnp.einsum("ak,ar->kr", flat, weights, precision=HIGH)
    mttkrp_c = lax.psum_scatter(partial_c, ("ia", "ja"), scatter_dimension=0, tiled=True)
    new_c = solve_rows(mttkrp_c, gram_a * gram_b_new)
    return (new_a[None], new_b[None], new_c[None])


def solution(mesh):
    return jax.shard_map(
        on_device,
        mesh=mesh,
        in_specs=(P("ia", "ja", "ka"), P("ja", ("ia", "ka"), None), P("ka", ("ia", "ja"), None)),
        out_specs=(
            P("ia", ("ja", "ka"), None),
            P("ja", ("ia", "ka"), None),
            P("ka", ("ia", "ja"), None),
        ),
        check_vma=False,
    )
```

profile of v0, /device:TPU:1, one launch (start us, length us, event | category | flops | bytes accessed | tf_op | source)
XLA Modules:
  0.0 2473.8 jit_solution(18030219943348131204)
XLA Ops:
  7.2 0.7 copy.19
  7.9 37.9 %all_gather.13 = f32[1,64,256]{2,0,1:T(1,128)S(1)} all-gather(f32[1,4,256]{2,0,1:T(1,128)S(1)} %copy.19), channel_id=1, replica_groups=mesh['ia'=8,'ja'=16,'ka'=2] {'ia','ka'}, dimensions={1}, use_global_device_ids=true | all-gather | bytes 69632 | tf_op jit(solution)/shard_map/all_gather | solution.py:20
  45.9 0.7 copy.18
  46.6 160.8 %all_gather.12 = f32[1,256,256]{2,0,1:T(1,128)S(1)} all-gather(f32[1,2,256]{2,0,1:T(1,128)S(1)} %copy.18), channel_id=1, replica_groups=mesh['ia'=8,'ja'=16,'ka'=2] {'ia','ja'}, dimensions={1}, use_global_device_ids=true | all-gather | bytes 264192 | tf_op jit(solution)/shard_map/all_gather | solution.py:21
  207.3 9.1 multiply_reduce_fusion
  216.4 0.8 copy.34
  217.3 1.1 fusion.48
  218.4 1.1 fusion.54
  219.6 0.6 all-reduce.18.cloned.1.call-start
  220.4 0.6 dynamic-slice.8
  221.6 100.2 %all-reduce.16.cloned.1.call-done = f32[128,256]{0,1:T(8,128)} async-done(((f32[128,256]{0,1:T(8,128)}), f32[128,256]{0,1:T(8,128)}) %all-reduce.16.cloned.1.call-update) | async-done | bytes 131088
  321.8 1.0 dynamic-slice_bitcast_fusion.2
  322.8 256.5 %all-reduce.22.cloned.1.call-done = (f32[256,256]{0,1:T(8,128)}, f32[256,256]{0,1:T(8,128)}) async-done(((f32[256,256]{0,1:T(8,128)}, f32[256,256]{0,1:T(8,128)}), (f32[256,256]{0,1:T(8,128)}, f32[256,256]{0,1:T(8,128)})) %all-reduce.22.cloned.1.call-update) | async-done | bytes 524304 | tf_op jit(solution)/shard_map/psum | solution.py:22
  579.3 1.1 mul.24
  580.5 11.7 cholesky.172
  592.3 9.8 custom-call.24
  602.6 11.7 cholesky.189
  614.4 0.6 compare_reduce_fusion.4
  616.4 4.2 while.6
  616.6 0.6 fusion.89
  617.2 1.4 bitcast_dynamic-update-slice_fusion.7
  618.6 0.6 fusion.89
  619.2 1.4 bitcast_dynamic-update-slice_fusion.7
  620.6 19.7 custom-call.25
  641.7 65.3 %all-gather.2 = f32[32,4,256]{2,1,0:T(4,128)S(1)} all-gather(f32[1,4,256]{2,1,0:T(4,128)S(1)} %fusion.53), channel_id=2, replica_groups=mesh['ia'=8,'ja'=16,'ka'=2] {'ja','ka'}, dimensions={0}, use_global_device_ids=true | all-gather | bytes 135168 | tf_op jit(solution)/shard_map/all_gather | solution.py:27
  707.0 21.5 fusion.5
  728.5 21.6 fusion
  750.2 1.1 fusion.52
  751.6 0.6 dynamic-slice.10
  752.8 0.6 dynamic-slice.12
  754.2 138.0 %all-reduce.18.cloned.1.call-done = f32[64,256]{0,1:T(8,128)} async-done(((f32[64,256]{0,1:T(8,128)}), f32[64,256]{0,1:T(8,128)}) %all-reduce.18.cloned.1.call-update) | async-done | bytes 65552
  892.2 1.0 dynamic-slice_bitcast_fusion.1
  893.2 261.6 %all-reduce.12.cloned.1.call-done = f32[256,256]{0,1:T(8,128)} async-done(((f32[256,256]{0,1:T(8,128)}), f32[256,256]{0,1:T(8,128)}) %all-reduce.12.cloned.1.call-update) | async-done | bytes 262160 | tf_op jit(solution)/shard_map/psum | solution.py:28
  1154.8 1.1 mul.25
  1156.1 11.7 cholesky.206
  1167.9 9.8 custom-call.26
  1178.2 11.7 cholesky.223
  1189.9 0.6 compare_reduce_fusion.3
  1190.5 0.7 compare_reduce_fusion.2
  1192.7 4.1 while.7
  1192.7 0.6 fusion.90
  1193.3 1.4 bitcast_dynamic-update-slice_fusion.8
  1194.7 0.6 fusion.90
  1195.3 1.4 bitcast_dynamic-update-slice_fusion.8
  1196.8 19.7 custom-call.27
  1217.9 1.2 fusion.50
  1219.0 34.4 %all-gather.3 = f32[16,4,256]{2,1,0:T(4,128)S(1)} all-gather(f32[1,4,256]{2,1,0:T(4,128)S(1)} %fusion.51), channel_id=3, replica_groups=mesh['ia'=8,'ja'=16,'ka'=2] {'ia','ka'}, dimensions={0}, use_global_device_ids=true | all-gather | bytes 69632 | tf_op jit(solution)/shard_map/all_gather | solution.py:33
  1253.7 15.0 fusion.10
  1268.7 236.6 %all-reduce.14.cloned.1.call-done = f32[256,256]{0,1:T(8,128)} async-done(((f32[256,256]{0,1:T(8,128)}), f32[256,256]{0,1:T(8,128)}) %all-reduce.14.cloned.1.call-update) | async-done | bytes 262160 | tf_op jit(solution)/shard_map/psum | solution.py:34
  1505.3 1.0 mul.26
  1506.5 12.1 cholesky.240
  1518.6 9.8 custom-call.28
  1528.9 11.7 cholesky.257
  1540.7 0.6 compare_reduce_fusion.1
  1541.3 0.7 compare_reduce_fusion
  1543.4 4.3 while.5
  1543.6 0.6 fusion.88
  1544.2 1.4 bitcast_dynamic-update-slice_fusion.6
  1545.7 0.6 fusion.88
  1546.3 1.4 bitcast_dynamic-update-slice_fusion.6
  1547.7 19.7 custom-call.20
  1567.4 896.4 %all-reduce.20.cloned.1.call-done = f32[256,256]{0,1:T(8,128)} async-done(((f32[256,256]{0,1:T(8,128)}), f32[256,256]{0,1:T(8,128)}) %all-reduce.20.cloned.1.call-update) | async-done | bytes 262160
  2463.8 1.0 dynamic-slice_bitcast_fusion
  2466.2 0.6 maximum_bitcast_fusion
  (94 shorter events, 7.7 us)
Async XLA Ops:
  7.2 213.2 %copy-start.8 = (u32[256]{0:T(256)S(1)}, u32[256]{0:T(256)}, u32[]{:S(2)}) copy-start(u32[256]{0:T(256)} %constant.125) | copy-start | bytes 3076
  7.2 210.1 %copy-start.2 = (f32[1,4,256]{2,1,0:T(4,128)S(1)}, f32[1,4,256]{2,1,0:T(4,128)}, u32[]{:S(2)}) copy-start(f32[1,4,256]{2,1,0:T(4,128)} %param.7) | copy-start | bytes 12292
  7.2 211.2 %copy-start.5 = (f32[1,2,256]{2,1,0:T(2,128)S(1)}, f32[1,2,256]{2,1,0:T(2,128)}, u32[]{:S(2)}) copy-start(f32[1,2,256]{2,1,0:T(2,128)} %param.8) | copy-start | bytes 6148
  7.2 314.6 %all-reduce.16.cloned.1.call-start = ((), (), s32[]{:S(2)}) async-start(), calls=%async_computation.2 | async-start | bytes 262144
  217.2 362.1 %all-reduce.22.cloned.1.call-start = ((), (), s32[]{:S(2)}) async-start(), calls=%async_computation.5 | async-start | bytes 1048576 | tf_op jit(solution)/shard_map/psum | solution.py:22
  219.6 672.7 %all-reduce.18.cloned.1.call-start = ((), (), s32[]{:S(2)}) async-start(), calls=%async_computation.3 | async-start | bytes 262144
  641.7 86.8 %copy-start.3 = (f32[1,4,256]{2,1,0:T(4,128)}, f32[1,4,256]{2,1,0:T(4,128)S(1)}, u32[]{:S(2)}) copy-start(f32[1,4,256]{2,1,0:T(4,128)S(1)} %fusion.53) | copy-start | bytes 12292
  728.5 23.1 copy-start.7
  728.5 24.3 copy-start.6
  728.5 426.3 %copy-start = (f32[256,256]{0,1:T(8,128)S(1)}, f32[256,256]{0,1:T(8,128)}, u32[]{:S(2)}) copy-start(f32[256,256]{0,1:T(8,128)} %get-tuple-element.54) | copy-start | bytes 786436
  750.1 404.7 %all-reduce.12.cloned.1.call-start = ((), (), s32[]{:S(2)}) async-start(), calls=%async_computation | async-start | bytes 524288 | tf_op jit(solution)/shard_map/psum | solution.py:28
  751.3 754.0 %all-reduce.14.cloned.1.call-start = ((), (), s32[]{:S(2)}) async-start(), calls=%async_computation.1 | async-start | bytes 524288 | tf_op jit(solution)/shard_map/psum | solution.py:34
  1154.8 350.5 %copy-start.1 = (f32[256,256]{0,1:T(8,128)S(1)}, f32[256,256]{0,1:T(8,128)}, u32[]{:S(2)}) copy-start(f32[256,256]{0,1:T(8,128)} %all-reduce.12.cloned.1.call-done) | copy-start | bytes 786436
  1217.8 1249.0 %copy-start.4 = (f32[1,4,256]{2,1,0:T(4,128)}, f32[1,4,256]{2,1,0:T(4,128)S(1)}, u32[]{:S(2)}) copy-start(f32[1,4,256]{2,1,0:T(4,128)S(1)} %fusion.51) | copy-start | bytes 12292
  1253.5 1210.4 %all-reduce.20.cloned.1.call-start = ((), (), s32[]{:S(2)}) async-start(), calls=%async_computation.4 | async-start | bytes 524288
Sparse Core Ops, SparseCore 0:
  217.3 104.4 all-reduce.15
  328.4 250.8 all-reduce.21
  750.3 141.9 all-reduce.17
  897.5 257.2 all-reduce.11
  1253.6 251.6 all-reduce.13
  1507.8 955.9 all-reduce.19
where the time goes:
time: 2480 us; the launch traced here: 2470 us
  waiting for transfers between devices  1890 us (76%)
  blocking collectives  298 us (12%)
  other arithmetic  167 us (7%)
  matrix products  77.1 us (3%)
    unnamed x9, waiting for transfers between devices  1130 us
    psum x1, waiting for transfers between devices, on_device(): gram_a = lax.psum(gram_of(new_a), ('ia', 'ja', 'ka'))  262 us
    psum x1, waiting for transfers between devices, on_device(): lax.psum((gram_of(factor_b[0]), gram_of(factor_c[0])), ('ia', 'ja', 'ka'))  256 us
    psum x1, waiting for transfers between devices, on_device(): gram_b_new = lax.psum(gram_of(new_b), ('ia', 'ja', 'ka'))  237 us
    all_gather x1, blocking collectives, on_device(): c_slice = lax.all_gather(factor_c, ('ia', 'ja'), axis=1, tiled=True)[0]  161 us
    another operation x20, other arithmetic, solve_rows(): factor = jnp.linalg.cholesky(gram)  104 us
    all_gather x1, blocking collectives, on_device(): a_slice = lax.all_gather(new_a[None], ('ja', 'ka'), axis=1, tiled=True)[0]  65.3 us
    another operation x7, other arithmetic, solve_rows(): return jax.scipy.linalg.cho_solve((factor, True), right.T).T  59.1 us
  transfers between devices with their start and end apart: 6, of which 6 were waited for; matrix products, arithmetic and copies ran while one was open for 3% of the time, Pallas kernels for 0%

commit v1 on v0

v1 whole, which is shorter than its diff:
```python
import functools

import jax
import jax.numpy as jnp
from jax import lax
from jax.experimental import pallas as pl
from jax.experimental.pallas import tpu as pltpu
from jax.sharding import PartitionSpec as P

HIGH = lax.Precision.HIGHEST
MESH = pl.DeviceIdType.MESH
F32 = jnp.float32
BF16 = jnp.bfloat16
NB = 32


def dot_f32(x, y, dims):
    return lax.dot_general(x, y, (dims, ((), ())), precision=HIGH, preferred_element_type=F32)


def dot_bf16(x, y, dims):
    return lax.dot_general(x, y, (dims, ((), ())), preferred_element_type=F32)


def split2(x):
    high = x.astype(BF16)
    return high, (x - high.astype(F32)).astype(BF16)


def split3(x):
    first = x.astype(BF16)
    rest = x - first.astype(F32)
    second = rest.astype(BF16)
    return first, second, (rest - second.astype(F32)).astype(BF16)


def invert(s_ref):
    n = s_ref.shape[0]
    rows_at = lax.broadcasted_iota(jnp.int32, (NB, n), 0)
    lanes_at = lax.broadcasted_iota(jnp.int32, (NB, n), 1)

    for block in range(n // NB):
        low = block * NB
        old = s_ref[low : low + NB, :]
        panel = old
        for j in range(NB):
            column = panel[:, low + j : low + j + 1]
            inverse = 1.0 / panel[j : j + 1, low + j : low + j + 1]
            here = lanes_at == low + j
            pivot_row = jnp.where(here[:1], 1.0, panel[j : j + 1, :]) * inverse
            panel = jnp.where(here, 0.0, panel)
            panel = jnp.where(rows_at == j, pivot_row, panel - column * pivot_row)
        signed = jnp.where(lanes_at < low, -old, jnp.where(lanes_at < low + NB, 0.0, old))
        x1, x2, x3 = split3(signed)
        y1, y2, y3 = split3(panel)
        update = dot_bf16(
            jnp.concatenate([x1, x1, x2, x2, x1, x3], axis=0),
            jnp.concatenate([y1, y2, y1, y2, y3, y1], axis=0),
            ((0,), (0,)),
        )
        all_lanes = lax.broadcasted_iota(jnp.int32, (n, n), 1)
        inside = (all_lanes >= low) & (all_lanes < low + NB)
        s_ref[...] = jnp.where(inside, 0.0, s_ref[...]) - update
        s_ref[low : low + NB, :] = panel


def kernel(
    n_ia, n_ja, n_ka,
    t_hbm, b_ref, c_ref,
    a_out, b_out, c_out,
    t_ref, thi, tlo, p_ref,
    c_in1, c_in2, c_all, b_in, b_all,
    gb_mine, gb_in, gc_mine, gc_in, gc_rows, ga_rows,
    g_send, g_all,
    a_parts, a_in, a_own, a_in2, a_slice, ga_mine, ga_in,
    bm_parts, bm_in, b_own, b_in2, b_slice, gb2_mine, gb2_in,
    cm_mine, cm_parts, cm_in, cm_sum, cm_in2,
    t_sem, send_sem, recv_sem,
):
    i_dev, j_dev, k_dev = t_hbm.shape
    rank = c_ref.shape[-1]
    ia, ja, ka = lax.axis_index("ia"), lax.axis_index("ja"), lax.axis_index("ka")
    n_g, n_h = n_ja * n_ka, n_ia * n_ka
    g_at = ja * n_ka + ka
    h_at = ia * n_ka + ka
    g_tall = rank // n_g

    def device(z, j, k):
        return {"ia": z, "ja": j, "ka": k}

    def plane(step):
        at = lax.rem(g_at + step, n_g)
        return at, device(ia, at // n_ka, lax.rem(at, n_ka))

    def column(step):
        at = lax.rem(ia + step, n_ia)
        return at, device(at, ja, ka)

    def column_pair(step):
        at = lax.rem(h_at + step, n_h)
        return at, device(at // n_ka, ja, lax.rem(at, n_ka))

    def row(step):
        at = lax.rem(ja + step, n_ja)
        return at, device(ia, at, ka)

    def send(phase, n, peer, source, target):
        def body(step, carry):
            at, who = peer(step)
            pltpu.make_async_remote_copy(
                src_ref=source(at), dst_ref=target(at), send_sem=send_sem.at[phase],
                recv_sem=recv_sem.at[phase], device_id=who, device_id_type=MESH,
            ).start()
            return carry
        lax.fori_loop(1, n, body, 0)

    def done(phase, ref, sem):
        pltpu.make_async_copy(ref, ref, sem.at[phase]).wait()

    chunks = t_sem.shape[0]
    i_chunk = i_dev // chunks

    def load(at):
        span = pl.ds(at * i_chunk, i_chunk)
        return pltpu.make_async_copy(t_hbm.at[span], t_ref.at[span], t_sem.at[at])

    for at in range(chunks):
        load(at).start()

    barrier = pltpu.get_barrier_semaphore()

    def greet_plane(step, carry):
        pl.semaphore_signal(barrier, inc=1, device_id=plane(step)[1], device_id_type=MESH)
        return carry

    def greet_column(step, carry):
        z = lax.rem(ia + step, n_ia)
        for k in range(n_ka):
            pl.semaphore_signal(barrier, inc=1, device_id=device(z, ja, k), device_id_type=MESH)
        return carry

    lax.fori_loop(1, n_g, greet_plane, 0)
    lax.fori_loop(1, n_ia, greet_column, 0)
    pl.semaphore_wait(barrier, n_g - 1 + (n_ia - 1) * n_ka)

    send(0, n_ia, column, lambda at: c_ref.at[0], lambda at: c_in1.at[ia])
    send(1, n_h, column_pair, lambda at: b_ref.at[0], lambda at: b_in.at[h_at])
    c_in1[ia] = c_ref[0]
    b_in[h_at] = b_ref[0]
    done(0, c_in1.at[pl.ds(0, n_ia - 1)], recv_sem)
    send(2, n_ja, row, lambda at: c_in1, lambda at: c_in2.at[ja])
    c_in2[ja] = c_in1[...]

    for at in range(chunks):
        load(at).wait()

        def split_one(i, carry):
            high, low = split2(t_ref[i])
            thi[i] = high
            tlo[i] = low
            return carry
        lax.fori_loop(at * i_chunk, (at + 1) * i_chunk, split_one, 0)

    done(1, b_in.at[pl.ds(0, n_h - 1)], recv_sem)
    for h in range(n_h):
        b_all[4 * h : 4 * h + 4, :] = b_in[h]
    gb_mine[...] = dot_f32(b_all[...], b_all[...], ((0,), (0,)))

    def rows_of(ref, at):
        return ref.at[pl.ds(pl.multiple_of(at * g_tall, 8), g_tall)]

    send(3, n_ja, row, lambda at: rows_of(gb_mine, at * n_ka + ka), lambda at: gb_in.at[ja])
    done(2, c_in2.at[pl.ds(0, n_ja - 1)], recv_sem)
    for z in range(n_ia):
        for j in range(n_ja):
            low = 2 * (z * n_ja + j)
            c_all[low : low + 2, :] = c_in2[j, z]
    gc_mine[...] = dot_f32(c_all[...], c_all[...], ((0,), (0,)))

    def other(step):
        at = lax.rem(ka + step, n_ka)
        return at, device(ia, ja, at)

    send(4, n_ka, other, lambda at: rows_of(gc_mine, ja * n_ka + at), lambda at: gc_in.at[ka])

    chi, clo = split2(c_all[...])
    per = 8
    b_whole = b_all[...]

    def first(step, carry):
        span = pl.ds(step * per, per)
        left_hi = thi[span].reshape(per * j_dev, k_dev)
        left_lo = tlo[span].reshape(per * j_dev, k_dev)
        inner = dot_bf16(left_hi, chi, ((1,), (0,))) + (
            dot_bf16(left_hi, clo, ((1,), (0,))) + dot_bf16(left_lo, chi, ((1,), (0,)))
        )
        inner = inner.reshape(per, j_dev, rank)
        p_ref[span] = inner
        summed = jnp.sum(inner * b_whole[None], axis=1)
        a_parts[pl.ds(step * (per // 4), per // 4)] = summed.reshape(per // 4, 4, rank)
        return carry
    lax.fori_loop(0, i_dev // per, first, 0)

    send(5, n_g, plane, lambda at: a_parts.at[at], lambda at: a_in.at[g_at])
    a_in[g_at] = a_parts[g_at]

    def gather_gram(phase, slot, rows):
        g_send[slot] = rows
        rows_of(g_all.at[slot], g_at)[...] = rows
        send(phase, n_g, plane, lambda at: g_send.at[slot], lambda at: rows_of(g_all.at[slot], g_at))

    gb_in[ja] = rows_of(gb_mine, g_at)[...]
    gc_in[ka] = rows_of(gc_mine, g_at)[...]
    done(3, gb_in.at[pl.ds(0, n_ja - 1)], recv_sem)
    done(4, gc_in.at[pl.ds(0, n_ka - 1)], recv_sem)
    gc_rows[...] = jnp.sum(gc_in[...], axis=0)
    gather_gram(6, 0, jnp.sum(gb_in[...], axis=0) * gc_rows[...])
    done(6, g_all.at[0, pl.ds(0, rank - g_tall)], recv_sem)
    invert(g_all.at[0])
    done(5, a_in.at[pl.ds(0, n_g - 1)], recv_sem)
    own = dot_f32(jnp.sum(a_in[...], axis=0), g_all[0], ((1,), (0,)))
    a_out[0] = own
    a_own[...] = own

    a_in2[g_at] = own
    send(7, n_g, plane, lambda at: a_own, lambda at: a_in2.at[g_at])
    done(7, a_in2.at[pl.ds(0, n_g - 1)], recv_sem)
    for g in range(n_g):
        a_slice[4 * g : 4 * g + 4, :] = a_in2[g]
    ga_mine[...] = dot_f32(a_slice[...], a_slice[...], ((0,), (0,)))
    send(8, n_ia, column, lambda at: rows_of(ga_mine, g_at), lambda at: ga_in.at[ia])
    ga_in[ia] = rows_of(ga_mine, g_at)[...]

    def second(step, total):
        for e in range(4):
            i = step * 4 + e
            total = total + p_ref[i] * a_slice[pl.ds(i, 1), :]
        return total
    sums = lax.fori_loop(0, i_dev // 4, second, jnp.zeros((j_dev, rank), F32))
    for h in range(n_h):
        bm_parts[h] = sums[4 * h : 4 * h + 4]
    send(9, n_h, column_pair, lambda at: bm_parts.at[at], lambda at: bm_in.at[h_at])
    bm_in[h_at] = bm_parts[h_at]
    done(8, ga_in.at[pl.ds(0, n_ia - 1)], recv_sem)
    ga_rows[...] = jnp.sum(ga_in[...], axis=0)
    gather_gram(10, 1, ga_rows[...] * gc_rows[...])
    done(10, g_all.at[1, pl.ds(0, rank - g_tall)], recv_sem)
    invert(g_all.at[1])
    done(9, bm_in.at[pl.ds(0, n_h - 1)], recv_sem)
    own = dot_f32(jnp.sum(bm_in[...], axis=0), g_all[1], ((1,), (0,)))
    b_out[0] = own
    b_own[...] = own

    b_in2[h_at] = own
    send(11, n_h, column_pair, lambda at: b_own, lambda at: b_in2.at[h_at])
    done(11, b_in2.at[pl.ds(0, n_h - 1)], recv_sem)
    for h in range(n_h):
        b_slice[4 * h : 4 * h + 4, :] = b_in2[h]
    gb2_mine[...] = dot_f32(b_slice[...], b_slice[...], ((0,), (0,)))
    send(12, n_ja, row, lambda at: rows_of(gb2_mine, at * n_ka + ka), lambda at: gb2_in.at[ja])
    gb2_in[ja] = rows_of(gb2_mine, g_at)[...]

    b_now = b_slice[...]
    cm_mine[...] = jnp.zeros_like(cm_mine)

    def third(step, carry):
        span = pl.ds(step * per, per)
        weights = (a_slice[pl.ds(pl.multiple_of(step * per, per), per), :][:, None, :] * b_now[None]).reshape(per * j_dev, rank)
        whi, wlo = split2(weights)
        left_hi = thi[span].reshape(per * j_dev, k_dev)
        left_lo = tlo[span].reshape(per * j_dev, k_dev)
        cm_mine[...] += dot_bf16(left_hi, whi, ((0,), (0,))) + (
            dot_bf16(left_hi, wlo, ((0,), (0,))) + dot_bf16(left_lo, whi, ((0,), (0,)))
        )
        return carry
    lax.fori_loop(0, i_dev // per, third, 0)
    for z in range(n_ia):
        for j in range(n_ja):
            low = 2 * (z * n_ja + j)
            cm_parts[j, z] = cm_mine[low : low + 2, :]
    send(13, n_ja, row, lambda at: cm_parts.at[at], lambda at: cm_in.at[ja])
    cm_in[ja] = cm_parts[ja]
    done(12, gb2_in.at[pl.ds(0, n_ja - 1)], recv_sem)
    gather_gram(14, 2, jnp.sum(gb2_in[...], axis=0) * ga_rows[...])
    done(13, cm_in.at[pl.ds(0, n_ja - 1)], recv_sem)
    cm_sum[...] = jnp.sum(cm_in[...], axis=0)
    send(15, n_ia, column, lambda at: cm_sum.at[at], lambda at: cm_in2.at[ia])
    cm_in2[ia] = cm_sum[ia]
    done(14, g_all.at[2, pl.ds(0, rank - g_tall)], recv_sem)
    invert(g_all.at[2])
    done(15, cm_in2.at[pl.ds(0, n_ia - 1)], recv_sem)
    c_out[0] = dot_f32(jnp.sum(cm_in2[...], axis=0), g_all[2], ((1,), (0,)))

    sent = (
        c_in1.at[pl.ds(0, n_ia - 1)], b_in.at[pl.ds(0, n_h - 1)], c_in2.at[pl.ds(0, n_ja - 1)], gb_in.at[pl.ds(0, n_ja - 1)],
        gc_in.at[pl.ds(0, n_ka - 1)], a_in.at[pl.ds(0, n_g - 1)], g_all.at[0, pl.ds(0, rank - g_tall)], a_in2.at[pl.ds(0, n_g - 1)],
        ga_in.at[pl.ds(0, n_ia - 1)], bm_in.at[pl.ds(0, n_h - 1)], g_all.at[1, pl.ds(0, rank - g_tall)], b_in2.at[pl.ds(0, n_h - 1)],
        gb2_in.at[pl.ds(0, n_ja - 1)], cm_in.at[pl.ds(0, n_ja - 1)], g_all.at[2, pl.ds(0, rank - g_tall)], cm_in2.at[pl.ds(0, n_ia - 1)],
    )
    for phase, ref in enumerate(sent):
        done(phase, ref, send_sem)


def solution(mesh):
    n_ia, n_ja, n_ka = mesh.shape["ia"], mesh.shape["ja"], mesh.shape["ka"]
    n_g, n_h = n_ja * n_ka, n_ia * n_ka

    def on_device(tensor, factor_b, factor_c):
        i_dev, j_dev, k_dev = tensor.shape
        rank = factor_b.shape[-1]
        tall = rank // n_g

        def vmem(*shape, dtype=F32):
            return pltpu.VMEM(shape, dtype)

        square = (rank, rank)
        return pl.pallas_call(
            functools.partial(kernel, n_ia, n_ja, n_ka),
            out_shape=(
                jax.ShapeDtypeStruct((1, 4, rank), F32),
                jax.ShapeDtypeStruct((1, 4, rank), F32),
                jax.ShapeDtypeStruct((1, 2, rank), F32),
            ),
            in_specs=[pl.BlockSpec(memory_space=pl.ANY)] + [pl.BlockSpec(memory_space=pltpu.VMEM)] * 2,
            out_specs=(pl.BlockSpec(memory_space=pltpu.VMEM),) * 3,
            scratch_shapes=[
                vmem(i_dev, j_dev, k_dev), vmem(i_dev, j_dev, k_dev, dtype=BF16), vmem(i_dev, j_dev, k_dev, dtype=BF16),
                vmem(i_dev, j_dev, rank),
                vmem(n_ia, 2, rank), vmem(n_ja, n_ia, 2, rank), vmem(k_dev, rank), vmem(n_h, 4, rank), vmem(j_dev, rank),
                vmem(*square), vmem(n_ja, tall, rank), vmem(*square), vmem(n_ka, tall, rank), vmem(tall, rank), vmem(tall, rank),
                vmem(3, tall, rank), vmem(3, *square),
                vmem(n_g, 4, rank), vmem(n_g, 4, rank), vmem(4, rank), vmem(n_g, 4, rank), vmem(i_dev, rank), vmem(*square), vmem(n_ia, tall, rank),
                vmem(n_h, 4, rank), vmem(n_h, 4, rank), vmem(4, rank), vmem(n_h, 4, rank), vmem(j_dev, rank), vmem(*square), vmem(n_ja, tall, rank),
                vmem(k_dev, rank), vmem(n_ja, n_ia, 2, rank), vmem(n_ja, n_ia, 2, rank), vmem(n_ia, 2, rank), vmem(n_ia, 2, rank),
                pltpu.SemaphoreType.DMA((8,)), pltpu.SemaphoreType.DMA((16,)), pltpu.SemaphoreType.DMA((16,)),
            ],
            compiler_params=pltpu.CompilerParams(
                collective_id=0, has_side_effects=True, vmem_limit_bytes=56 * 1024 * 1024
            ),
        )(tensor, factor_b, factor_c)

    return jax.shard_map(
        on_device,
        mesh=mesh,
        in_specs=(P("ia", "ja", "ka"), P("ja", ("ia", "ka"), None), P("ka", ("ia", "ja"), None)),
        out_specs=(
            P("ia", ("ja", "ka"), None),
            P("ja", ("ia", "ka"), None),
            P("ka", ("ia", "ja"), None),
        ),
        check_vma=False,
    )
```

time: 2480 us -> 151 us (0.06)
  waiting for transfers between devices: 1890 us -> 0 us
  blocking collectives: 298 us -> 0 us
  other arithmetic: 167 us -> 0 us
  Pallas kernels: 0 us -> 146 us
  matrix products: 77.1 us -> 0 us
    unnamed x9 -> x0, waiting for transfers between devices: 1130 us -> none
    psum x3 -> x0, waiting for transfers between devices: 755 us -> none  [the longest x1 262 us: on_device(): gram_a = lax.psum(gram_of(new_a), ('ia', 'ja', 'ka'))]
    all_gather x4 -> x0, blocking collectives: 298 us -> none  [the longest x1 161 us: on_device(): c_slice = lax.all_gather(factor_c, ('ia', 'ja'), axis=1, tiled=True)[0]]
    another operation x27 -> x0, other arithmetic: 163 us -> none  [the longest x20 104 us: solve_rows(): factor = jnp.linalg.cholesky(gram)]
    pallas_call x0 -> x1, Pallas kernels: none -> 146 us  [on_device(): pl.pallas_call(functools.partial(kernel, n_ia, n_ja, n_ka), out_shape=(ja...]
    dot_general x8 -> x0, matrix products: 71.6 us -> none  [the longest x1 21.6 us: on_device(): partial_b = jnp.einsum('jkr,kr->jr', inner, c_slice, precision=HIGH)]
  transfers between devices with their start and end apart: 6 -> 0, of which waited for: 6 -> 0; matrix products, arithmetic and copies ran while one was open for 3% -> 0% of each run, Pallas kernels for 0% -> 0%
where the time goes in v1:
time: 151 us
  Pallas kernels  146 us (97%)
  local copies, waits for them, and re-layouts  3.77 us (2%)
    pallas_call x1, Pallas kernels, on_device(): pl.pallas_call(functools.partial(kernel, n_ia, n_ja, n_ka), out_shape=(ja...  146 us
    unnamed x3, local copies, waits for them, and re-layouts  3.77 us

profile of v1, /device:TPU:1, one launch (start us, length us, event | category | flops | bytes accessed | tf_op | source)
XLA Modules:
  0.0 150.8 jit_solution(16802865208360021798)
XLA Ops:
  0.6 146.4 %shard_map.58 = (f32[1,4,256]{2,1,0:T(4,128)}, f32[1,4,256]{2,1,0:T(4,128)}, f32[1,2,256]{2,1,0:T(2,128)}) custom-call(f32[128,64,256]{2,1,0:T(8,128)} %t_hbm.1, f32[1,4,256]{2,1,0:T(4,128)} %b_ref.1, f32[1,2,256]{2,1,0:T(2,128)} %c_ref.1), custom_call_target="tpu_custom_call" | custom-call | tf_op jit(solution)/shard_map/pallas_call | solution.py:317
  147.0 1.3 copy.9
  148.3 1.3 copy.10
  149.5 1.2 copy.11

commit v2 on v1

--- a/solution.py
+++ b/solution.py
@@ -34,22 +34,71 @@
     return first, second, (rest - second.astype(F32)).astype(BF16)
 
 
-def invert(s_ref):
+def spread(value, at):
+    return jnp.broadcast_to(value[at : at + 1, :], value.shape)
+
+
+def eliminate(old, low, steps):
+    n = old.shape[1]
+    tall, halves, per = old.shape[0] // 8, n // 128, steps // 8
+    rows = lax.broadcasted_iota(jnp.int32, (8, 128), 0)
+    lanes = lax.broadcasted_iota(jnp.int32, (8, 128), 1)
+    parts = [[old[8 * q : 8 * q + 8, 128 * w : 128 * w + 128] for w in range(halves)] for q in range(tall)]
+
+    def lane(q, at):
+        return jnp.broadcast_to(parts[q][at // 128][:, at % 128 : at % 128 + 1], (8, 128))
+
+    for group in range(tall // per):
+        base = low + steps * group
+        mine = range(group * per, (group + 1) * per)
+        half, first = base // 128, base % 128
+        inside = (lanes >= first) & (lanes < first + steps)
+        own = {(q, c): lane(q, base + c) for q in mine for c in range(steps)}
+        for q in mine:
+            unit = jnp.where(lanes - first == rows + 8 * (q - group * per), 1.0, 0.0)
+            parts[q][half] = jnp.where(inside, unit, parts[q][half])
+        pivot = spread(own[mine[0], 0], 0)
+        for j in range(steps):
+            at, r = group * per + j // 8, j % 8
+            here = rows == r
+            across = {c: spread(own[at, c], r) for c in range(j + 1, steps)}
+            inverse = 1.0 / pivot
+            if j + 1 < steps:
+                then, rn = group * per + (j + 1) // 8, (j + 1) % 8
+                pivot = spread(own[then, j + 1], rn) - (spread(own[then, j], rn) * across[j + 1]) * inverse
+            pivot_row = [spread(parts[at][w], r) for w in range(halves)]
+            for q in mine:
+                factor = own[q, j] * inverse
+                if q == at:
+                    factor = jnp.where(here, -inverse, factor)
+                for w in range(halves):
+                    kept = jnp.where(here, 0.0, parts[q][w]) if q == at else parts[q][w]
+                    parts[q][w] = kept - factor * pivot_row[w]
+                for c in range(j + 1, steps):
+                    kept = jnp.where(here, 0.0, own[q, c]) if q == at else own[q, c]
+                    own[q, c] = kept - factor * across[c]
+        done_rows = [[spread(parts[group * per + c // 8][w], c % 8) for w in range(halves)] for c in range(steps)]
+        for q in range(tall):
+            if q in mine:
+                continue
+            factors = [lane(q, base + c) for c in range(steps)]
+            parts[q][half] = jnp.where(inside, 0.0, parts[q][half])
+            for w in range(halves):
+                terms = [factors[c] * done_rows[c][w] for c in range(steps)]
+                while len(terms) > 1:
+                    terms = [x + y for x, y in zip(terms[::2], terms[1::2])]
+                parts[q][w] = parts[q][w] - terms[0]
+    return jnp.concatenate([jnp.concatenate(part, axis=1) for part in parts], axis=0)
+
+
+def invert(s_ref, blocks):
     n = s_ref.shape[0]
-    rows_at = lax.broadcasted_iota(jnp.int32, (NB, n), 0)
     lanes_at = lax.broadcasted_iota(jnp.int32, (NB, n), 1)
-
-    for block in range(n // NB):
+    all_lanes = lax.broadcasted_iota(jnp.int32, (n, n), 1)
+    for block in blocks:
         low = block * NB
         old = s_ref[low : low + NB, :]
-        panel = old
-        for j in range(NB):
-            column = panel[:, low + j : low + j + 1]
-            inverse = 1.0 / panel[j : j + 1, low + j : low + j + 1]
-            here = lanes_at == low + j
-            pivot_row = jnp.where(here[:1], 1.0, panel[j : j + 1, :]) * inverse
-            panel = jnp.where(here, 0.0, panel)
-            panel = jnp.where(rows_at == j, pivot_row, panel - column * pivot_row)
+        panel = eliminate(old, low, 16)
         signed = jnp.where(lanes_at < low, -old, jnp.where(lanes_at < low + NB, 0.0, old))
         x1, x2, x3 = split3(signed)
         y1, y2, y3 = split3(panel)
@@ -58,7 +107,6 @@
             jnp.concatenate([y1, y2, y1, y2, y3, y1], axis=0),
             ((0,), (0,)),
         )
-        all_lanes = lax.broadcasted_iota(jnp.int32, (n, n), 1)
         inside = (all_lanes >= low) & (all_lanes < low + NB)
         s_ref[...] = jnp.where(inside, 0.0, s_ref[...]) - update
         s_ref[low : low + NB, :] = panel
@@ -74,7 +122,7 @@
     g_send, g_all,
     a_parts, a_in, a_own, a_in2, a_slice, ga_mine, ga_in,
     bm_parts, bm_in, b_own, b_in2, b_slice, gb2_mine, gb2_in,
-    cm_mine, cm_parts, cm_in, cm_sum, cm_in2,
+    cm_mine, cm_parts, cm_in, cm_sum, cm_in2, a_mine, b_mine,
     t_sem, send_sem, recv_sem,
 ):
     i_dev, j_dev, k_dev = t_hbm.shape
@@ -84,6 +132,7 @@
     g_at = ja * n_ka + ka
     h_at = ia * n_ka + ka
     g_tall = rank // n_g
+    n_blocks = rank // NB
 
     def device(z, j, k):
         return {"ia": z, "ja": j, "ka": k}
@@ -184,7 +233,7 @@
     send(4, n_ka, other, lambda at: rows_of(gc_mine, ja * n_ka + at), lambda at: gc_in.at[ka])
 
     chi, clo = split2(c_all[...])
-    per = 8
+    per = 16
     b_whole = b_all[...]
 
     def first(step, carry):
@@ -215,18 +264,17 @@
     done(4, gc_in.at[pl.ds(0, n_ka - 1)], recv_sem)
     gc_rows[...] = jnp.sum(gc_in[...], axis=0)
     gather_gram(6, 0, jnp.sum(gb_in[...], axis=0) * gc_rows[...])
-    done(6, g_all.at[0, pl.ds(0, rank - g_tall)], recv_sem)
-    invert(g_all.at[0])
     done(5, a_in.at[pl.ds(0, n_g - 1)], recv_sem)
-    own = dot_f32(jnp.sum(a_in[...], axis=0), g_all[0], ((1,), (0,)))
-    a_out[0] = own
+    own = jnp.sum(a_in[...], axis=0)
     a_own[...] = own
-
     a_in2[g_at] = own
     send(7, n_g, plane, lambda at: a_own, lambda at: a_in2.at[g_at])
+    done(6, g_all.at[0, pl.ds(0, rank - g_tall)], recv_sem)
+    invert(g_all.at[0], range(n_blocks))
     done(7, a_in2.at[pl.ds(0, n_g - 1)], recv_sem)
     for g in range(n_g):
         a_slice[4 * g : 4 * g + 4, :] = a_in2[g]
+    a_slice[...] = dot_f32(a_slice[...], g_all[0], ((1,), (0,)))
     ga_mine[...] = dot_f32(a_slice[...], a_slice[...], ((0,), (0,)))
     send(8, n_ia, column, lambda at: rows_of(ga_mine, g_at), lambda at: ga_in.at[ia])
     ga_in[ia] = rows_of(ga_mine, g_at)[...]
@@ -244,22 +292,27 @@
     done(8, ga_in.at[pl.ds(0, n_ia - 1)], recv_sem)
     ga_rows[...] = jnp.sum(ga_in[...], axis=0)
     gather_gram(10, 1, ga_rows[...] * gc_rows[...])
-    done(10, g_all.at[1, pl.ds(0, rank - g_tall)], recv_sem)
-    invert(g_all.at[1])
     done(9, bm_in.at[pl.ds(0, n_h - 1)], recv_sem)
-    own = dot_f32(jnp.sum(bm_in[...], axis=0), g_all[1], ((1,), (0,)))
-    b_out[0] = own
+    own = jnp.sum(bm_in[...], axis=0)
     b_own[...] = own
-
     b_in2[h_at] = own
     send(11, n_h, column_pair, lambda at: b_own, lambda at: b_in2.at[h_at])
+    for g in range(n_g):
+        a_mine[g] = a_slice[4 * g : 4 * g + 4, :]
+    a_out[0] = a_mine[g_at]
+    done(10, g_all.at[1, pl.ds(0, rank - g_tall)], recv_sem)
+    invert(g_all.at[1], range(n_blocks))
     done(11, b_in2.at[pl.ds(0, n_h - 1)], recv_sem)
     for h in range(n_h):
         b_slice[4 * h : 4 * h + 4, :] = b_in2[h]
+    b_slice[...] = dot_f32(b_slice[...], g_all[1], ((1,), (0,)))
     gb2_mine[...] = dot_f32(b_slice[...], b_slice[...], ((0,), (0,)))
     send(12, n_ja, row, lambda at: rows_of(gb2_mine, at * n_ka + ka), lambda at: gb2_in.at[ja])
     gb2_in[ja] = rows_of(gb2_mine, g_at)[...]
 
+    for h in range(n_h):
+        b_mine[h] = b_slice[4 * h : 4 * h + 4, :]
+    b_out[0] = b_mine[h_at]
     b_now = b_slice[...]
     cm_mine[...] = jnp.zeros_like(cm_mine)
 
@@ -287,7 +340,7 @@
     send(15, n_ia, column, lambda at: cm_sum.at[at], lambda at: cm_in2.at[ia])
     cm_in2[ia] = cm_sum[ia]
     done(14, g_all.at[2, pl.ds(0, rank - g_tall)], recv_sem)
-    invert(g_all.at[2])
+    invert(g_all.at[2], range(n_blocks))
     done(15, cm_in2.at[pl.ds(0, n_ia - 1)], recv_sem)
     c_out[0] = dot_f32(jnp.sum(cm_in2[...], axis=0), g_all[2], ((1,), (0,)))
 
@@ -332,6 +385,7 @@
                 vmem(n_g, 4, rank), vmem(n_g, 4, rank), vmem(4, rank), vmem(n_g, 4, rank), vmem(i_dev, rank), vmem(*square), vmem(n_ia, tall, rank),
                 vmem(n_h, 4, rank), vmem(n_h, 4, rank), vmem(4, rank), vmem(n_h, 4, rank), vmem(j_dev, rank), vmem(*square), vmem(n_ja, tall, rank),
                 vmem(k_dev, rank), vmem(n_ja, n_ia, 2, rank), vmem(n_ja, n_ia, 2, rank), vmem(n_ia, 2, rank), vmem(n_ia, 2, rank),
+                vmem(n_g, 4, rank), vmem(n_h, 4, rank),
                 pltpu.SemaphoreType.DMA((8,)), pltpu.SemaphoreType.DMA((16,)), pltpu.SemaphoreType.DMA((16,)),
             ],
             compiler_params=pltpu.CompilerParams(

time: 151 us -> 90.6 us (0.60)
  Pallas kernels: 146 us -> 86 us
    pallas_call x1, Pallas kernels: 146 us -> 86 us  [on_device(): pl.pallas_call(functools.partial(kernel, n_ia, n_ja, n_ka), out_shape=(ja...]
where the time goes in v2:
time: 90.6 us; the launch traced here: 90.4 us
  Pallas kernels  86 us (95%)
  local copies, waits for them, and re-layouts  3.77 us (4%)
    pallas_call x1, Pallas kernels, on_device(): pl.pallas_call(functools.partial(kernel, n_ia, n_ja, n_ka), out_shape=(ja...  86 us
    unnamed x3, local copies, waits for them, and re-layouts  3.77 us

profile of v2, /device:TPU:1, one launch (start us, length us, event | category | flops | bytes accessed | tf_op | source)
XLA Modules:
  0.0 90.4 jit_solution(2079716098635637028)
XLA Ops:
  0.6 86.0 %shard_map.58 = (f32[1,4,256]{2,1,0:T(4,128)}, f32[1,4,256]{2,1,0:T(4,128)}, f32[1,2,256]{2,1,0:T(2,128)}) custom-call(f32[128,64,256]{2,1,0:T(8,128)} %t_hbm.1, f32[1,4,256]{2,1,0:T(4,128)} %b_ref.1, f32[1,2,256]{2,1,0:T(2,128)} %c_ref.1), custom_call_target="tpu_custom_call" | custom-call | tf_op jit(solution)/shard_map/pallas_call | solution.py:370
  86.6 1.3 %copy.9 = f32[1,4,256]{2,1,0:T(4,128)} copy(f32[1,4,256]{2,1,0:T(4,128)} %get-tuple-element.6) | data formatting | bytes 8192
  87.9 1.3 %copy.10 = f32[1,4,256]{2,1,0:T(4,128)} copy(f32[1,4,256]{2,1,0:T(4,128)} %get-tuple-element.7) | data formatting | bytes 8192
  89.1 1.2 %copy.11 = f32[1,2,256]{2,1,0:T(2,128)} copy(f32[1,2,256]{2,1,0:T(2,128)} %get-tuple-element.8) | data formatting | bytes 4096

commit v3 on v2

--- a/solution.py
+++ b/solution.py
@@ -153,13 +153,16 @@
         at = lax.rem(ja + step, n_ja)
         return at, device(ia, at, ka)
 
+    def start(phase, source, target, who):
+        pltpu.make_async_remote_copy(
+            src_ref=source, dst_ref=target, send_sem=send_sem.at[phase],
+            recv_sem=recv_sem.at[phase], device_id=who, device_id_type=MESH,
+        ).start()
+
     def send(phase, n, peer, source, target):
         def body(step, carry):
             at, who = peer(step)
-            pltpu.make_async_remote_copy(
-                src_ref=source(at), dst_ref=target(at), send_sem=send_sem.at[phase],
-                recv_sem=recv_sem.at[phase], device_id=who, device_id_type=MESH,
-            ).start()
+            start(phase, source(at), target(at), who)
             return carry
         lax.fori_loop(1, n, body, 0)
 
@@ -236,8 +239,11 @@
     per = 16
     b_whole = b_all[...]
 
+    pieces, steps = per // 4, i_dev // per
+
     def first(step, carry):
-        span = pl.ds(step * per, per)
+        at = lax.rem(g_at // pieces + 1 + step, steps)
+        span = pl.ds(at * per, per)
         left_hi = thi[span].reshape(per * j_dev, k_dev)
         left_lo = tlo[span].reshape(per * j_dev, k_dev)
         inner = dot_bf16(left_hi, chi, ((1,), (0,))) + (
@@ -246,24 +252,30 @@
         inner = inner.reshape(per, j_dev, rank)
         p_ref[span] = inner
         summed = jnp.sum(inner * b_whole[None], axis=1)
-        a_parts[pl.ds(step * (per // 4), per // 4)] = summed.reshape(per // 4, 4, rank)
+        a_parts[pl.ds(at * pieces, pieces)] = summed.reshape(pieces, 4, rank)
+        for e in range(pieces):
+            to = at * pieces + e
+
+            @pl.when(to != g_at)
+            def _():
+                start(5, a_parts.at[to], a_in.at[g_at], device(ia, to // n_ka, lax.rem(to, n_ka)))
         return carry
-    lax.fori_loop(0, i_dev // per, first, 0)
-
-    send(5, n_g, plane, lambda at: a_parts.at[at], lambda at: a_in.at[g_at])
-    a_in[g_at] = a_parts[g_at]
 
     def gather_gram(phase, slot, rows):
         g_send[slot] = rows
         rows_of(g_all.at[slot], g_at)[...] = rows
         send(phase, n_g, plane, lambda at: g_send.at[slot], lambda at: rows_of(g_all.at[slot], g_at))
 
+    lax.fori_loop(0, steps // 2, first, 0)
     gb_in[ja] = rows_of(gb_mine, g_at)[...]
     gc_in[ka] = rows_of(gc_mine, g_at)[...]
     done(3, gb_in.at[pl.ds(0, n_ja - 1)], recv_sem)
     done(4, gc_in.at[pl.ds(0, n_ka - 1)], recv_sem)
     gc_rows[...] = jnp.sum(gc_in[...], axis=0)
     gather_gram(6, 0, jnp.sum(gb_in[...], axis=0) * gc_rows[...])
+    lax.fori_loop(steps // 2, steps, first, 0)
+    a_in[g_at] = a_parts[g_at]
+
     done(5, a_in.at[pl.ds(0, n_g - 1)], recv_sem)
     own = jnp.sum(a_in[...], axis=0)
     a_own[...] = own
@@ -326,15 +338,17 @@
             dot_bf16(left_hi, wlo, ((0,), (0,))) + dot_bf16(left_lo, whi, ((0,), (0,)))
         )
         return carry
-    lax.fori_loop(0, i_dev // per, third, 0)
+    early = steps * 3 // 4
+    lax.fori_loop(0, early, third, 0)
+    done(12, gb2_in.at[pl.ds(0, n_ja - 1)], recv_sem)
+    gather_gram(14, 2, jnp.sum(gb2_in[...], axis=0) * ga_rows[...])
+    lax.fori_loop(early, steps, third, 0)
     for z in range(n_ia):
         for j in range(n_ja):
             low = 2 * (z * n_ja + j)
             cm_parts[j, z] = cm_mine[low : low + 2, :]
     send(13, n_ja, row, lambda at: cm_parts.at[at], lambda at: cm_in.at[ja])
     cm_in[ja] = cm_parts[ja]
-    done(12, gb2_in.at[pl.ds(0, n_ja - 1)], recv_sem)
-    gather_gram(14, 2, jnp.sum(gb2_in[...], axis=0) * ga_rows[...])
     done(13, cm_in.at[pl.ds(0, n_ja - 1)], recv_sem)
     cm_sum[...] = jnp.sum(cm_in[...], axis=0)
     send(15, n_ia, column, lambda at: cm_sum.at[at], lambda at: cm_in2.at[ia])
@@ -354,6 +368,17 @@
         done(phase, ref, send_sem)
 
 
+def hand_over(a_ref, b_ref, c_ref, a_out, b_out, c_out, sem):
+    copies = [
+        pltpu.make_async_copy(source, target, sem.at[at])
+        for at, (source, target) in enumerate(((a_ref, a_out), (b_ref, b_out), (c_ref, c_out)))
+    ]
+    for copy in copies:
+        copy.start()
+    for copy in copies:
+        copy.wait()
+
+
 def solution(mesh):
     n_ia, n_ja, n_ka = mesh.shape["ia"], mesh.shape["ja"], mesh.shape["ka"]
     n_g, n_h = n_ja * n_ka, n_ia * n_ka
@@ -367,13 +392,10 @@
             return pltpu.VMEM(shape, dtype)
 
         square = (rank, rank)
-        return pl.pallas_call(
+        outs = tuple(jax.ShapeDtypeStruct((1, rows, rank), F32) for rows in (4, 4, 2))
+        found = pl.pallas_call(
             functools.partial(kernel, n_ia, n_ja, n_ka),
-            out_shape=(
-                jax.ShapeDtypeStruct((1, 4, rank), F32),
-                jax.ShapeDtypeStruct((1, 4, rank), F32),
-                jax.ShapeDtypeStruct((1, 2, rank), F32),
-            ),
+            out_shape=outs,
             in_specs=[pl.BlockSpec(memory_space=pl.ANY)] + [pl.BlockSpec(memory_space=pltpu.VMEM)] * 2,
             out_specs=(pl.BlockSpec(memory_space=pltpu.VMEM),) * 3,
             scratch_shapes=[
@@ -392,6 +414,13 @@
                 collective_id=0, has_side_effects=True, vmem_limit_bytes=56 * 1024 * 1024
             ),
         )(tensor, factor_b, factor_c)
+        return pl.pallas_call(
+            hand_over,
+            out_shape=outs,
+            in_specs=[pl.BlockSpec(memory_space=pl.ANY)] * 3,
+            out_specs=(pl.BlockSpec(memory_space=pl.ANY),) * 3,
+            scratch_shapes=[pltpu.SemaphoreType.DMA((3,))],
+        )(*found)
 
     return jax.shard_map(
         on_device,

time: 90.6 us -> 84.9 us (0.937)
  local copies, waits for them, and re-layouts: 3.77 us -> 0 us
  Pallas kernels: 86 us -> 84 us
    unnamed x3 -> x0, local copies, waits for them, and re-layouts: 3.77 us -> none
    pallas_call x1 -> x2, Pallas kernels: 86 us -> 84 us  [the longest x1 82.5 us: on_device(): pl.pallas_call(functools.partial(kernel, n_ia, n_ja, n_ka), out_shape=out...]
where the time goes in v3:
time: 84.9 us; the launch traced here: 84.8 us
  Pallas kernels  84 us (99%)
    pallas_call x1, Pallas kernels, on_device(): pl.pallas_call(functools.partial(kernel, n_ia, n_ja, n_ka), out_shape=out...  82.5 us

profile of v3, /device:TPU:1, one launch (start us, length us, event | category | flops | bytes accessed | tf_op | source)
XLA Modules:
  0.0 84.8 jit_solution(8114569096412359950)
XLA Ops:
  0.6 82.5 %shard_map.58 = (f32[1,4,256]{2,1,0:T(4,128)}, f32[1,4,256]{2,1,0:T(4,128)}, f32[1,2,256]{2,1,0:T(2,128)}) custom-call(f32[128,64,256]{2,1,0:T(8,128)} %t_hbm.1, f32[1,4,256]{2,1,0:T(4,128)} %b_ref.1, f32[1,2,256]{2,1,0:T(2,128)} %c_ref.1), custom_call_target="tpu_custom_call" | custom-call | tf_op jit(solution)/shard_map/pallas_call | solution.py:396
  83.2 1.4 %shard_map.59 = (f32[1,4,256]{2,1,0:T(4,128)}, f32[1,4,256]{2,1,0:T(4,128)}, f32[1,2,256]{2,1,0:T(2,128)}) custom-call(f32[1,4,256]{2,1,0:T(4,128)} %get-tuple-element.6.a_ref, f32[1,4,256]{2,1,0:T(4,128)} %get-tuple-element.7.b_ref, f32[1,2,256]{2,1,0:T(2,128)} %get-tuple-element.8.c_ref), custom_call_target="tpu_custom_call" | custom-call | tf_op jit(solution)/shard_map/pallas_call | solution.py:417

commit v4 on v3

--- a/solution.py
+++ b/solution.py
@@ -12,6 +12,8 @@
 F32 = jnp.float32
 BF16 = jnp.bfloat16
 NB = 32
+NEAR = [(1, 0, 0), (-1, 0, 0), (0, 1, 0), (0, -1, 0), (1, 1, 0), (1, -1, 0), (-1, 1, 0), (-1, -1, 0), (2, 0, 0), (0, 2, 0)]
+ACROSS = [(0, 0, 1), (1, 0, -1), (-1, 0, 1), (0, 1, -1), (0, -1, 1)]
 
 
 def dot_f32(x, y, dims):
@@ -159,6 +161,18 @@
             recv_sem=recv_sem.at[phase], device_id=who, device_id_type=MESH,
         ).start()
 
+    def piece(z, j, k):
+        odd = lax.rem(z, 2)
+        return lax.rem(j + odd * (n_ja // 2), n_ja) * n_ka + lax.rem(k + odd, n_ka)
+
+    piece_at = piece(ia, ja, ka)
+    chip_x, chip_y, core = ja // 4, ka * 2 + lax.rem(ja // 2, 2), lax.rem(ja, 2)
+
+    def chip(offset, other):
+        x, y = lax.rem(chip_x + offset[0] + 4, 4), lax.rem(chip_y + offset[1] + 4, 4)
+        z, c = lax.rem(ia + offset[2] + n_ia, n_ia), lax.rem(core + other, 2)
+        return device(z, x * 4 + lax.rem(y, 2) * 2 + c, y // 2)
+
     def send(phase, n, peer, source, target):
         def body(step, carry):
             at, who = peer(step)
@@ -193,7 +207,10 @@
 
     lax.fori_loop(1, n_g, greet_plane, 0)
     lax.fori_loop(1, n_ia, greet_column, 0)
-    pl.semaphore_wait(barrier, n_g - 1 + (n_ia - 1) * n_ka)
+    beyond = [(offset, other) for offset in ACROSS for other in (0, 1) if (offset[:2], other) != ((0, 0), 0)]
+    for (x, y, z), other in beyond:
+        pl.semaphore_signal(barrier, inc=1, device_id=chip((-x, -y, -z), other), device_id_type=MESH)
+    pl.semaphore_wait(barrier, n_g - 1 + (n_ia - 1) * n_ka + len(beyond))
 
     send(0, n_ia, column, lambda at: c_ref.at[0], lambda at: c_in1.at[ia])
     send(1, n_h, column_pair, lambda at: b_ref.at[0], lambda at: b_in.at[h_at])
@@ -221,7 +238,7 @@
     def rows_of(ref, at):
         return ref.at[pl.ds(pl.multiple_of(at * g_tall, 8), g_tall)]
 
-    send(3, n_ja, row, lambda at: rows_of(gb_mine, at * n_ka + ka), lambda at: gb_in.at[ja])
+    send(3, n_ja, row, lambda at: rows_of(gb_mine, piece(ia, at, ka)), lambda at: gb_in.at[ja])
     done(2, c_in2.at[pl.ds(0, n_ja - 1)], recv_sem)
     for z in range(n_ia):
         for j in range(n_ja):
@@ -233,10 +250,10 @@
         at = lax.rem(ka + step, n_ka)
         return at, device(ia, ja, at)
 
-    send(4, n_ka, other, lambda at: rows_of(gc_mine, ja * n_ka + at), lambda at: gc_in.at[ka])
+    send(4, n_ka, other, lambda at: rows_of(gc_mine, piece(ia, ja, at)), lambda at: gc_in.at[ka])
 
     chi, clo = split2(c_all[...])
-    per = 16
+    per = 32
     b_whole = b_all[...]
 
     pieces, steps = per // 4, i_dev // per
@@ -263,12 +280,13 @@
 
     def gather_gram(phase, slot, rows):
         g_send[slot] = rows
-        rows_of(g_all.at[slot], g_at)[...] = rows
-        send(phase, n_g, plane, lambda at: g_send.at[slot], lambda at: rows_of(g_all.at[slot], g_at))
+        rows_of(g_all.at[slot], piece_at)[...] = rows
+        for offset, other in [((0, 0, 0), 1)] + [(offset, other) for offset in ACROSS + NEAR[::-1] for other in (0, 1)]:
+            start(phase, g_send.at[slot], rows_of(g_all.at[slot], piece_at), chip(offset, other))
 
     lax.fori_loop(0, steps // 2, first, 0)
-    gb_in[ja] = rows_of(gb_mine, g_at)[...]
-    gc_in[ka] = rows_of(gc_mine, g_at)[...]
+    gb_in[ja] = rows_of(gb_mine, piece_at)[...]
+    gc_in[ka] = rows_of(gc_mine, piece_at)[...]
     done(3, gb_in.at[pl.ds(0, n_ja - 1)], recv_sem)
     done(4, gc_in.at[pl.ds(0, n_ka - 1)], recv_sem)
     gc_rows[...] = jnp.sum(gc_in[...], axis=0)
@@ -288,8 +306,8 @@
         a_slice[4 * g : 4 * g + 4, :] = a_in2[g]
     a_slice[...] = dot_f32(a_slice[...], g_all[0], ((1,), (0,)))
     ga_mine[...] = dot_f32(a_slice[...], a_slice[...], ((0,), (0,)))
-    send(8, n_ia, column, lambda at: rows_of(ga_mine, g_at), lambda at: ga_in.at[ia])
-    ga_in[ia] = rows_of(ga_mine, g_at)[...]
+    send(8, n_ia, column, lambda at: rows_of(ga_mine, piece(at, ja, ka)), lambda at: ga_in.at[ia])
+    ga_in[ia] = rows_of(ga_mine, piece_at)[...]
 
     def second(step, total):
         for e in range(4):
@@ -319,8 +337,8 @@
         b_slice[4 * h : 4 * h + 4, :] = b_in2[h]
     b_slice[...] = dot_f32(b_slice[...], g_all[1], ((1,), (0,)))
     gb2_mine[...] = dot_f32(b_slice[...], b_slice[...], ((0,), (0,)))
-    send(12, n_ja, row, lambda at: rows_of(gb2_mine, at * n_ka + ka), lambda at: gb2_in.at[ja])
-    gb2_in[ja] = rows_of(gb2_mine, g_at)[...]
+    send(12, n_ja, row, lambda at: rows_of(gb2_mine, piece(ia, at, ka)), lambda at: gb2_in.at[ja])
+    gb2_in[ja] = rows_of(gb2_mine, piece_at)[...]
 
     for h in range(n_h):
         b_mine[h] = b_slice[4 * h : 4 * h + 4, :]

time: 84.9 us -> 82.4 us (0.971)
  Pallas kernels: 84 us -> 81.5 us
    pallas_call x1, Pallas kernels: 82.5 us -> 80 us  [on_device(): pl.pallas_call(functools.partial(kernel, n_ia, n_ja, n_ka), out_shape=out...]
where the time goes in v4:
time: 82.4 us; the launch traced here: 82.3 us
  Pallas kernels  81.5 us (99%)
    pallas_call x1, Pallas kernels, on_device(): pl.pallas_call(functools.partial(kernel, n_ia, n_ja, n_ka), out_shape=out...  80 us

profile of v4, /device:TPU:1, one launch (start us, length us, event | category | flops | bytes accessed | tf_op | source)
XLA Modules:
  0.0 82.3 jit_solution(16834922571802821318)
XLA Ops:
  0.6 80.0 %shard_map.58 = (f32[1,4,256]{2,1,0:T(4,128)}, f32[1,4,256]{2,1,0:T(4,128)}, f32[1,2,256]{2,1,0:T(2,128)}) custom-call(f32[128,64,256]{2,1,0:T(8,128)} %t_hbm.1, f32[1,4,256]{2,1,0:T(4,128)} %b_ref.1, f32[1,2,256]{2,1,0:T(2,128)} %c_ref.1), custom_call_target="tpu_custom_call" | custom-call | tf_op jit(solution)/shard_map/pallas_call | solution.py:414
  80.7 1.4 %shard_map.59 = (f32[1,4,256]{2,1,0:T(4,128)}, f32[1,4,256]{2,1,0:T(4,128)}, f32[1,2,256]{2,1,0:T(2,128)}) custom-call(f32[1,4,256]{2,1,0:T(4,128)} %get-tuple-element.6.a_ref, f32[1,4,256]{2,1,0:T(4,128)} %get-tuple-element.7.b_ref, f32[1,2,256]{2,1,0:T(2,128)} %get-tuple-element.8.c_ref), custom_call_target="tpu_custom_call" | custom-call | tf_op jit(solution)/shard_map/pallas_call | solution.py:435

commit v5 on v4

--- a/solution.py
+++ b/solution.py
@@ -139,20 +139,23 @@
     def device(z, j, k):
         return {"ia": z, "ja": j, "ka": k}
 
+    def far_first(step, n):
+        return n // 2 + step // 2 * (2 * lax.rem(step, 2) - 1)
+
     def plane(step):
-        at = lax.rem(g_at + step, n_g)
+        at = lax.rem(g_at + far_first(step, n_g), n_g)
         return at, device(ia, at // n_ka, lax.rem(at, n_ka))
 
     def column(step):
-        at = lax.rem(ia + step, n_ia)
+        at = lax.rem(ia + far_first(step, n_ia), n_ia)
         return at, device(at, ja, ka)
 
     def column_pair(step):
-        at = lax.rem(h_at + step, n_h)
+        at = lax.rem(h_at + far_first(step, n_h), n_h)
         return at, device(at // n_ka, ja, lax.rem(at, n_ka))
 
     def row(step):
-        at = lax.rem(ja + step, n_ja)
+        at = lax.rem(ja + far_first(step, n_ja), n_ja)
         return at, device(ia, at, ka)
 
     def start(phase, source, target, who):
@@ -200,24 +203,29 @@
         return carry
 
     def greet_column(step, carry):
-        z = lax.rem(ia + step, n_ia)
+        z = column(step)[0]
         for k in range(n_ka):
             pl.semaphore_signal(barrier, inc=1, device_id=device(z, ja, k), device_id_type=MESH)
         return carry
 
+    lax.fori_loop(1, n_ia, greet_column, 0)
     lax.fori_loop(1, n_g, greet_plane, 0)
-    lax.fori_loop(1, n_ia, greet_column, 0)
     beyond = [(offset, other) for offset in ACROSS for other in (0, 1) if (offset[:2], other) != ((0, 0), 0)]
     for (x, y, z), other in beyond:
         pl.semaphore_signal(barrier, inc=1, device_id=chip((-x, -y, -z), other), device_id_type=MESH)
     pl.semaphore_wait(barrier, n_g - 1 + (n_ia - 1) * n_ka + len(beyond))
 
-    send(0, n_ia, column, lambda at: c_ref.at[0], lambda at: c_in1.at[ia])
+    for step in (4, 3, 5, 2, 6, 1, 7):
+        who = device(lax.rem(ia + step, n_ia), ja, ka)
+        start(0 if step in (1, 2, 6, 7) else 16, c_ref.at[0], c_in1.at[(10 - step) % 8], who)
     send(1, n_h, column_pair, lambda at: b_ref.at[0], lambda at: b_in.at[h_at])
-    c_in1[ia] = c_ref[0]
+    c_in1[2] = c_ref[0]
     b_in[h_at] = b_ref[0]
-    done(0, c_in1.at[pl.ds(0, n_ia - 1)], recv_sem)
-    send(2, n_ja, row, lambda at: c_in1, lambda at: c_in2.at[ja])
+    near, rest = pl.ds(0, 5), pl.ds(5, 3)
+    done(0, c_in1.at[pl.ds(0, 4)], recv_sem)
+    send(2, n_ja, row, lambda at: c_in1.at[near], lambda at: c_in2.at[ja, near])
+    done(16, c_in1.at[pl.ds(0, 3)], recv_sem)
+    send(17, n_ja, row, lambda at: c_in1.at[rest], lambda at: c_in2.at[ja, rest])
     c_in2[ja] = c_in1[...]
 
     for at in range(chunks):
@@ -239,12 +247,14 @@
         return ref.at[pl.ds(pl.multiple_of(at * g_tall, 8), g_tall)]
 
     send(3, n_ja, row, lambda at: rows_of(gb_mine, piece(ia, at, ka)), lambda at: gb_in.at[ja])
-    done(2, c_in2.at[pl.ds(0, n_ja - 1)], recv_sem)
-    for z in range(n_ia):
-        for j in range(n_ja):
-            low = 2 * (z * n_ja + j)
-            c_all[low : low + 2, :] = c_in2[j, z]
-    gc_mine[...] = dot_f32(c_all[...], c_all[...], ((0,), (0,)))
+    for phase, slots in ((2, range(5)), (17, range(5, 8))):
+        done(phase, c_in2.at[pl.ds(0, n_ja - 1), pl.ds(slots[0], len(slots))], recv_sem)
+        for slot in slots:
+            z = lax.rem(ia + slot + n_ia - 2, n_ia)
+            for j in range(n_ja):
+                c_all[z, 2 * j : 2 * j + 2, :] = c_in2[j, slot]
+    c_whole = c_all[...].reshape(k_dev, rank)
+    gc_mine[...] = dot_f32(c_whole, c_whole, ((0,), (0,)))
 
     def other(step):
         at = lax.rem(ka + step, n_ka)
@@ -252,11 +262,12 @@
 
     send(4, n_ka, other, lambda at: rows_of(gc_mine, piece(ia, ja, at)), lambda at: gc_in.at[ka])
 
-    chi, clo = split2(c_all[...])
+    chi, clo = split2(c_whole)
     per = 32
     b_whole = b_all[...]
 
     pieces, steps = per // 4, i_dev // per
+    early = steps * 3 // 4
 
     def first(step, carry):
         at = lax.rem(g_at // pieces + 1 + step, steps)
@@ -284,23 +295,24 @@
         for offset, other in [((0, 0, 0), 1)] + [(offset, other) for offset in ACROSS + NEAR[::-1] for other in (0, 1)]:
             start(phase, g_send.at[slot], rows_of(g_all.at[slot], piece_at), chip(offset, other))
 
-    lax.fori_loop(0, steps // 2, first, 0)
+    lax.fori_loop(0, early, first, 0)
     gb_in[ja] = rows_of(gb_mine, piece_at)[...]
     gc_in[ka] = rows_of(gc_mine, piece_at)[...]
     done(3, gb_in.at[pl.ds(0, n_ja - 1)], recv_sem)
     done(4, gc_in.at[pl.ds(0, n_ka - 1)], recv_sem)
     gc_rows[...] = jnp.sum(gc_in[...], axis=0)
     gather_gram(6, 0, jnp.sum(gb_in[...], axis=0) * gc_rows[...])
-    lax.fori_loop(steps // 2, steps, first, 0)
+    lax.fori_loop(early, steps, first, 0)
     a_in[g_at] = a_parts[g_at]
 
+    done(6, g_all.at[0, pl.ds(0, rank - g_tall)], recv_sem)
+    invert(g_all.at[0], range(3))
     done(5, a_in.at[pl.ds(0, n_g - 1)], recv_sem)
     own = jnp.sum(a_in[...], axis=0)
     a_own[...] = own
     a_in2[g_at] = own
     send(7, n_g, plane, lambda at: a_own, lambda at: a_in2.at[g_at])
-    done(6, g_all.at[0, pl.ds(0, rank - g_tall)], recv_sem)
-    invert(g_all.at[0], range(n_blocks))
+    invert(g_all.at[0], range(3, n_blocks))
     done(7, a_in2.at[pl.ds(0, n_g - 1)], recv_sem)
     for g in range(n_g):
         a_slice[4 * g : 4 * g + 4, :] = a_in2[g]
@@ -356,7 +368,6 @@
             dot_bf16(left_hi, wlo, ((0,), (0,))) + dot_bf16(left_lo, whi, ((0,), (0,)))
         )
         return carry
-    early = steps * 3 // 4
     lax.fori_loop(0, early, third, 0)
     done(12, gb2_in.at[pl.ds(0, n_ja - 1)], recv_sem)
     gather_gram(14, 2, jnp.sum(gb2_in[...], axis=0) * ga_rows[...])
@@ -367,20 +378,22 @@
             cm_parts[j, z] = cm_mine[low : low + 2, :]
     send(13, n_ja, row, lambda at: cm_parts.at[at], lambda at: cm_in.at[ja])
     cm_in[ja] = cm_parts[ja]
+    done(14, g_all.at[2, pl.ds(0, rank - g_tall)], recv_sem)
+    invert(g_all.at[2], range(n_blocks // 2))
     done(13, cm_in.at[pl.ds(0, n_ja - 1)], recv_sem)
     cm_sum[...] = jnp.sum(cm_in[...], axis=0)
     send(15, n_ia, column, lambda at: cm_sum.at[at], lambda at: cm_in2.at[ia])
     cm_in2[ia] = cm_sum[ia]
-    done(14, g_all.at[2, pl.ds(0, rank - g_tall)], recv_sem)
-    invert(g_all.at[2], range(n_blocks))
+    invert(g_all.at[2], range(n_blocks // 2, n_blocks))
     done(15, cm_in2.at[pl.ds(0, n_ia - 1)], recv_sem)
     c_out[0] = dot_f32(jnp.sum(cm_in2[...], axis=0), g_all[2], ((1,), (0,)))
 
     sent = (
-        c_in1.at[pl.ds(0, n_ia - 1)], b_in.at[pl.ds(0, n_h - 1)], c_in2.at[pl.ds(0, n_ja - 1)], gb_in.at[pl.ds(0, n_ja - 1)],
+        c_in1.at[pl.ds(0, 4)], b_in.at[pl.ds(0, n_h - 1)], c_in2.at[pl.ds(0, n_ja - 1), near], gb_in.at[pl.ds(0, n_ja - 1)],
         gc_in.at[pl.ds(0, n_ka - 1)], a_in.at[pl.ds(0, n_g - 1)], g_all.at[0, pl.ds(0, rank - g_tall)], a_in2.at[pl.ds(0, n_g - 1)],
         ga_in.at[pl.ds(0, n_ia - 1)], bm_in.at[pl.ds(0, n_h - 1)], g_all.at[1, pl.ds(0, rank - g_tall)], b_in2.at[pl.ds(0, n_h - 1)],
         gb2_in.at[pl.ds(0, n_ja - 1)], cm_in.at[pl.ds(0, n_ja - 1)], g_all.at[2, pl.ds(0, rank - g_tall)], cm_in2.at[pl.ds(0, n_ia - 1)],
+        c_in1.at[pl.ds(0, 3)], c_in2.at[pl.ds(0, n_ja - 1), rest],
     )
     for phase, ref in enumerate(sent):
         done(phase, ref, send_sem)
@@ -419,14 +432,14 @@
             scratch_shapes=[
                 vmem(i_dev, j_dev, k_dev), vmem(i_dev, j_dev, k_dev, dtype=BF16), vmem(i_dev, j_dev, k_dev, dtype=BF16),
                 vmem(i_dev, j_dev, rank),
-                vmem(n_ia, 2, rank), vmem(n_ja, n_ia, 2, rank), vmem(k_dev, rank), vmem(n_h, 4, rank), vmem(j_dev, rank),
+                vmem(n_ia, 2, rank), vmem(n_ja, n_ia, 2, rank), vmem(n_ia, k_dev // n_ia, rank), vmem(n_h, 4, rank), vmem(j_dev, rank),
                 vmem(*square), vmem(n_ja, tall, rank), vmem(*square), vmem(n_ka, tall, rank), vmem(tall, rank), vmem(tall, rank),
                 vmem(3, tall, rank), vmem(3, *square),
                 vmem(n_g, 4, rank), vmem(n_g, 4, rank), vmem(4, rank), vmem(n_g, 4, rank), vmem(i_dev, rank), vmem(*square), vmem(n_ia, tall, rank),
                 vmem(n_h, 4, rank), vmem(n_h, 4, rank), vmem(4, rank), vmem(n_h, 4, rank), vmem(j_dev, rank), vmem(*square), vmem(n_ja, tall, rank),
                 vmem(k_dev, rank), vmem(n_ja, n_ia, 2, rank), vmem(n_ja, n_ia, 2, rank), vmem(n_ia, 2, rank), vmem(n_ia, 2, rank),
                 vmem(n_g, 4, rank), vmem(n_h, 4, rank),
-                pltpu.SemaphoreType.DMA((8,)), pltpu.SemaphoreType.DMA((16,)), pltpu.SemaphoreType.DMA((16,)),
+                pltpu.SemaphoreType.DMA((8,)), pltpu.SemaphoreType.DMA((18,)), pltpu.SemaphoreType.DMA((18,)),
             ],
             compiler_params=pltpu.CompilerParams(
                 collective_id=0, has_side_effects=True, vmem_limit_bytes=56 * 1024 * 1024

time: 82.4 us -> 76.1 us (0.924)
  Pallas kernels: 81.5 us -> 75.2 us
    pallas_call x1, Pallas kernels: 80 us -> 73.7 us  [on_device(): pl.pallas_call(functools.partial(kernel, n_ia, n_ja, n_ka), out_shape=out...]
where the time goes in v5:
time: 76.1 us; the launch traced here: 76 us
  Pallas kernels  75.2 us (99%)
  between operations  0.82 us (1%)
    pallas_call x1, Pallas kernels, on_device(): pl.pallas_call(functools.partial(kernel, n_ia, n_ja, n_ka), out_shape=out...  73.7 us

profile of v5, /device:TPU:1, one launch (start us, length us, event | category | flops | bytes accessed | tf_op | source)
XLA Modules:
  0.0 76.0 jit_solution(6203495266304080979)
XLA Ops:
  0.6 73.7 %shard_map.58 = (f32[1,4,256]{2,1,0:T(4,128)}, f32[1,4,256]{2,1,0:T(4,128)}, f32[1,2,256]{2,1,0:T(2,128)}) custom-call(f32[128,64,256]{2,1,0:T(8,128)} %t_hbm.1, f32[1,4,256]{2,1,0:T(4,128)} %b_ref.1, f32[1,2,256]{2,1,0:T(2,128)} %c_ref.1), custom_call_target="tpu_custom_call" | custom-call | tf_op jit(solution)/shard_map/pallas_call | solution.py:427
  74.4 1.4 %shard_map.59 = (f32[1,4,256]{2,1,0:T(4,128)}, f32[1,4,256]{2,1,0:T(4,128)}, f32[1,2,256]{2,1,0:T(2,128)}) custom-call(f32[1,4,256]{2,1,0:T(4,128)} %get-tuple-element.6.a_ref, f32[1,4,256]{2,1,0:T(4,128)} %get-tuple-element.7.b_ref, f32[1,2,256]{2,1,0:T(2,128)} %get-tuple-element.8.c_ref), custom_call_target="tpu_custom_call" | custom-call | tf_op jit(solution)/shard_map/pallas_call | solution.py:448

commit v6 on v5

--- a/solution.py
+++ b/solution.py
@@ -45,7 +45,9 @@
     tall, halves, per = old.shape[0] // 8, n // 128, steps // 8
     rows = lax.broadcasted_iota(jnp.int32, (8, 128), 0)
     lanes = lax.broadcasted_iota(jnp.int32, (8, 128), 1)
+    wide = lax.broadcasted_iota(jnp.int32, (8, n), 1)
     parts = [[old[8 * q : 8 * q + 8, 128 * w : 128 * w + 128] for w in range(halves)] for q in range(tall)]
+    before, after = [], []
 
     def lane(q, at):
         return jnp.broadcast_to(parts[q][at // 128][:, at % 128 : at % 128 + 1], (8, 128))
@@ -55,6 +57,9 @@
         mine = range(group * per, (group + 1) * per)
         half, first = base // 128, base % 128
         inside = (lanes >= first) & (lanes < first + steps)
+        for q in mine:
+            whole = jnp.concatenate(parts[q], axis=1)
+            before.append(jnp.where(wide < base, -whole, jnp.where(wide < low + old.shape[0], 0.0, whole)))
         own = {(q, c): lane(q, base + c) for q in mine for c in range(steps)}
         for q in mine:
             unit = jnp.where(lanes - first == rows + 8 * (q - group * per), 1.0, 0.0)
@@ -79,10 +84,11 @@
                 for c in range(j + 1, steps):
                     kept = jnp.where(here, 0.0, own[q, c]) if q == at else own[q, c]
                     own[q, c] = kept - factor * across[c]
+        for q in mine:
+            whole = jnp.concatenate(parts[q], axis=1)
+            after.append(jnp.where((wide >= base + steps) & (wide < low + old.shape[0]), 0.0, whole))
         done_rows = [[spread(parts[group * per + c // 8][w], c % 8) for w in range(halves)] for c in range(steps)]
-        for q in range(tall):
-            if q in mine:
-                continue
+        for q in range((group + 1) * per, tall):
             factors = [lane(q, base + c) for c in range(steps)]
             parts[q][half] = jnp.where(inside, 0.0, parts[q][half])
             for w in range(halves):
@@ -90,28 +96,29 @@
                 while len(terms) > 1:
                     terms = [x + y for x, y in zip(terms[::2], terms[1::2])]
                 parts[q][w] = parts[q][w] - terms[0]
-    return jnp.concatenate([jnp.concatenate(part, axis=1) for part in parts], axis=0)
+    return jnp.concatenate(before, axis=0), jnp.concatenate(after, axis=0)
+
+
+def stacked(x, y):
+    x1, x2, x3 = split3(x)
+    y1, y2, y3 = split3(y)
+    return dot_bf16(
+        jnp.concatenate([x1, x1, x2, x2, x1, x3], axis=0),
+        jnp.concatenate([y1, y2, y1, y2, y3, y1], axis=0),
+        ((0,), (0,)),
+    )
 
 
 def invert(s_ref, blocks):
     n = s_ref.shape[0]
-    lanes_at = lax.broadcasted_iota(jnp.int32, (NB, n), 1)
     all_lanes = lax.broadcasted_iota(jnp.int32, (n, n), 1)
     for block in blocks:
         low = block * NB
-        old = s_ref[low : low + NB, :]
-        panel = eliminate(old, low, 16)
-        signed = jnp.where(lanes_at < low, -old, jnp.where(lanes_at < low + NB, 0.0, old))
-        x1, x2, x3 = split3(signed)
-        y1, y2, y3 = split3(panel)
-        update = dot_bf16(
-            jnp.concatenate([x1, x1, x2, x2, x1, x3], axis=0),
-            jnp.concatenate([y1, y2, y1, y2, y3, y1], axis=0),
-            ((0,), (0,)),
-        )
+        before, after = eliminate(s_ref[low : low + NB, :], low, 16)
+        update = stacked(before, after)
         inside = (all_lanes >= low) & (all_lanes < low + NB)
         s_ref[...] = jnp.where(inside, 0.0, s_ref[...]) - update
-        s_ref[low : low + NB, :] = panel
+        s_ref[low : low + NB, :] = after - update[low : low + NB, :]
 
 
 def kernel(
@@ -267,10 +274,8 @@
     b_whole = b_all[...]
 
     pieces, steps = per // 4, i_dev // per
-    early = steps * 3 // 4
-
-    def first(step, carry):
-        at = lax.rem(g_at // pieces + 1 + step, steps)
+
+    for at in range(steps):
         span = pl.ds(at * per, per)
         left_hi = thi[span].reshape(per * j_dev, k_dev)
         left_lo = tlo[span].reshape(per * j_dev, k_dev)
@@ -279,15 +284,9 @@
         )
         inner = inner.reshape(per, j_dev, rank)
         p_ref[span] = inner
-        summed = jnp.sum(inner * b_whole[None], axis=1)
-        a_parts[pl.ds(at * pieces, pieces)] = summed.reshape(pieces, 4, rank)
-        for e in range(pieces):
-            to = at * pieces + e
-
-            @pl.when(to != g_at)
-            def _():
-                start(5, a_parts.at[to], a_in.at[g_at], device(ia, to // n_ka, lax.rem(to, n_ka)))
-        return carry
+        a_parts[pl.ds(at * pieces, pieces)] = jnp.sum(inner * b_whole[None], axis=1).reshape(pieces, 4, rank)
+    send(5, n_g, plane, lambda at: a_parts.at[at], lambda at: a_in.at[g_at])
+    a_in[g_at] = a_parts[g_at]
 
     def gather_gram(phase, slot, rows):
         g_send[slot] = rows
@@ -295,29 +294,26 @@
         for offset, other in [((0, 0, 0), 1)] + [(offset, other) for offset in ACROSS + NEAR[::-1] for other in (0, 1)]:
             start(phase, g_send.at[slot], rows_of(g_all.at[slot], piece_at), chip(offset, other))
 
-    lax.fori_loop(0, early, first, 0)
     gb_in[ja] = rows_of(gb_mine, piece_at)[...]
     gc_in[ka] = rows_of(gc_mine, piece_at)[...]
     done(3, gb_in.at[pl.ds(0, n_ja - 1)], recv_sem)
     done(4, gc_in.at[pl.ds(0, n_ka - 1)], recv_sem)
     gc_rows[...] = jnp.sum(gc_in[...], axis=0)
     gather_gram(6, 0, jnp.sum(gb_in[...], axis=0) * gc_rows[...])
-    lax.fori_loop(early, steps, first, 0)
-    a_in[g_at] = a_parts[g_at]
-
-    done(6, g_all.at[0, pl.ds(0, rank - g_tall)], recv_sem)
-    invert(g_all.at[0], range(3))
+
     done(5, a_in.at[pl.ds(0, n_g - 1)], recv_sem)
     own = jnp.sum(a_in[...], axis=0)
     a_own[...] = own
     a_in2[g_at] = own
     send(7, n_g, plane, lambda at: a_own, lambda at: a_in2.at[g_at])
-    invert(g_all.at[0], range(3, n_blocks))
+    done(6, g_all.at[0, pl.ds(0, rank - g_tall)], recv_sem)
+    invert(g_all.at[0], range(n_blocks))
     done(7, a_in2.at[pl.ds(0, n_g - 1)], recv_sem)
     for g in range(n_g):
         a_slice[4 * g : 4 * g + 4, :] = a_in2[g]
     a_slice[...] = dot_f32(a_slice[...], g_all[0], ((1,), (0,)))
-    ga_mine[...] = dot_f32(a_slice[...], a_slice[...], ((0,), (0,)))
+    a_now = a_slice[...]
+    ga_mine[...] = stacked(a_now, a_now)
     send(8, n_ia, column, lambda at: rows_of(ga_mine, piece(at, ja, ka)), lambda at: ga_in.at[ia])
     ga_in[ia] = rows_of(ga_mine, piece_at)[...]
 
@@ -348,30 +344,26 @@
     for h in range(n_h):
         b_slice[4 * h : 4 * h + 4, :] = b_in2[h]
     b_slice[...] = dot_f32(b_slice[...], g_all[1], ((1,), (0,)))
-    gb2_mine[...] = dot_f32(b_slice[...], b_slice[...], ((0,), (0,)))
+    b_now = b_slice[...]
+    gb2_mine[...] = stacked(b_now, b_now)
     send(12, n_ja, row, lambda at: rows_of(gb2_mine, piece(ia, at, ka)), lambda at: gb2_in.at[ja])
     gb2_in[ja] = rows_of(gb2_mine, piece_at)[...]
 
     for h in range(n_h):
         b_mine[h] = b_slice[4 * h : 4 * h + 4, :]
     b_out[0] = b_mine[h_at]
-    b_now = b_slice[...]
-    cm_mine[...] = jnp.zeros_like(cm_mine)
-
-    def third(step, carry):
-        span = pl.ds(step * per, per)
-        weights = (a_slice[pl.ds(pl.multiple_of(step * per, per), per), :][:, None, :] * b_now[None]).reshape(per * j_dev, rank)
+    for at in range(steps):
+        span = pl.ds(at * per, per)
+        weights = (a_slice[span, :][:, None, :] * b_now[None]).reshape(per * j_dev, rank)
         whi, wlo = split2(weights)
         left_hi = thi[span].reshape(per * j_dev, k_dev)
         left_lo = tlo[span].reshape(per * j_dev, k_dev)
-        cm_mine[...] += dot_bf16(left_hi, whi, ((0,), (0,))) + (
+        product = dot_bf16(left_hi, whi, ((0,), (0,))) + (
             dot_bf16(left_hi, wlo, ((0,), (0,))) + dot_bf16(left_lo, whi, ((0,), (0,)))
         )
-        return carry
-    lax.fori_loop(0, early, third, 0)
+        cm_mine[...] = product if at == 0 else cm_mine[...] + product
     done(12, gb2_in.at[pl.ds(0, n_ja - 1)], recv_sem)
     gather_gram(14, 2, jnp.sum(gb2_in[...], axis=0) * ga_rows[...])
-    lax.fori_loop(early, steps, third, 0)
     for z in range(n_ia):
         for j in range(n_ja):
             low = 2 * (z * n_ja + j)

time: 76.1 us -> 83.6 us (1.099)
  Pallas kernels: 75.2 us -> 82.7 us
    pallas_call x1, Pallas kernels: 73.7 us -> 81.3 us  [on_device(): pl.pallas_call(functools.partial(kernel, n_ia, n_ja, n_ka), out_shape=out...]
where the time goes in v6:
time: 83.6 us; the launch traced here: 83.5 us
  Pallas kernels  82.7 us (99%)
    pallas_call x1, Pallas kernels, on_device(): pl.pallas_call(functools.partial(kernel, n_ia, n_ja, n_ka), out_shape=out...  81.3 us

profile of v6, /device:TPU:1, one launch (start us, length us, event | category | flops | bytes accessed | tf_op | source)
XLA Modules:
  0.0 83.5 jit_solution(10315456816134567268)
XLA Ops:
  0.6 81.3 %shard_map.58 = (f32[1,4,256]{2,1,0:T(4,128)}, f32[1,4,256]{2,1,0:T(4,128)}, f32[1,2,256]{2,1,0:T(2,128)}) custom-call(f32[128,64,256]{2,1,0:T(8,128)} %t_hbm.1, f32[1,4,256]{2,1,0:T(4,128)} %b_ref.1, f32[1,2,256]{2,1,0:T(2,128)} %c_ref.1), custom_call_target="tpu_custom_call" | custom-call | tf_op jit(solution)/shard_map/pallas_call | solution.py:419
  81.9 1.4 %shard_map.59 = (f32[1,4,256]{2,1,0:T(4,128)}, f32[1,4,256]{2,1,0:T(4,128)}, f32[1,2,256]{2,1,0:T(2,128)}) custom-call(f32[1,4,256]{2,1,0:T(4,128)} %get-tuple-element.6.a_ref, f32[1,4,256]{2,1,0:T(4,128)} %get-tuple-element.7.b_ref, f32[1,2,256]{2,1,0:T(2,128)} %get-tuple-element.8.c_ref), custom_call_target="tpu_custom_call" | custom-call | tf_op jit(solution)/shard_map/pallas_call | solution.py:440

commit v7 on v6

--- a/solution.py
+++ b/solution.py
@@ -40,30 +40,28 @@
     return jnp.broadcast_to(value[at : at + 1, :], value.shape)
 
 
-def eliminate(old, low, steps):
-    n = old.shape[1]
-    tall, halves, per = old.shape[0] // 8, n // 128, steps // 8
+def eliminate(own_half, other_half, first, processed, steps):
+    tall, per, end = NB // 8, steps // 8, first + NB
     rows = lax.broadcasted_iota(jnp.int32, (8, 128), 0)
     lanes = lax.broadcasted_iota(jnp.int32, (8, 128), 1)
-    wide = lax.broadcasted_iota(jnp.int32, (8, n), 1)
-    parts = [[old[8 * q : 8 * q + 8, 128 * w : 128 * w + 128] for w in range(halves)] for q in range(tall)]
+    parts = [[half[8 * q : 8 * q + 8, :] for half in (own_half, other_half)] for q in range(tall)]
     before, after = [], []
 
     def lane(q, at):
-        return jnp.broadcast_to(parts[q][at // 128][:, at % 128 : at % 128 + 1], (8, 128))
+        return jnp.broadcast_to(parts[q][0][:, at : at + 1], (8, 128))
 
     for group in range(tall // per):
-        base = low + steps * group
+        base = first + steps * group
         mine = range(group * per, (group + 1) * per)
-        half, first = base // 128, base % 128
-        inside = (lanes >= first) & (lanes < first + steps)
+        inside = (lanes >= base) & (lanes < base + steps)
         for q in mine:
-            whole = jnp.concatenate(parts[q], axis=1)
-            before.append(jnp.where(wide < base, -whole, jnp.where(wide < low + old.shape[0], 0.0, whole)))
+            near, far = parts[q]
+            near = jnp.where(lanes < base, -near, jnp.where(lanes < end, 0.0, near))
+            before.append(jnp.concatenate([near, jnp.where(processed, -far, far)], axis=1))
         own = {(q, c): lane(q, base + c) for q in mine for c in range(steps)}
         for q in mine:
-            unit = jnp.where(lanes - first == rows + 8 * (q - group * per), 1.0, 0.0)
-            parts[q][half] = jnp.where(inside, unit, parts[q][half])
+            unit = jnp.where(lanes - base == rows + 8 * (q - group * per), 1.0, 0.0)
+            parts[q][0] = jnp.where(inside, unit, parts[q][0])
         pivot = spread(own[mine[0], 0], 0)
         for j in range(steps):
             at, r = group * per + j // 8, j % 8
@@ -73,25 +71,25 @@
             if j + 1 < steps:
                 then, rn = group * per + (j + 1) // 8, (j + 1) % 8
                 pivot = spread(own[then, j + 1], rn) - (spread(own[then, j], rn) * across[j + 1]) * inverse
-            pivot_row = [spread(parts[at][w], r) for w in range(halves)]
+            pivot_row = [spread(parts[at][w], r) for w in range(2)]
             for q in mine:
                 factor = own[q, j] * inverse
                 if q == at:
                     factor = jnp.where(here, -inverse, factor)
-                for w in range(halves):
+                for w in range(2):
                     kept = jnp.where(here, 0.0, parts[q][w]) if q == at else parts[q][w]
                     parts[q][w] = kept - factor * pivot_row[w]
                 for c in range(j + 1, steps):
                     kept = jnp.where(here, 0.0, own[q, c]) if q == at else own[q, c]
                     own[q, c] = kept - factor * across[c]
         for q in mine:
-            whole = jnp.concatenate(parts[q], axis=1)
-            after.append(jnp.where((wide >= base + steps) & (wide < low + old.shape[0]), 0.0, whole))
-        done_rows = [[spread(parts[group * per + c // 8][w], c % 8) for w in range(halves)] for c in range(steps)]
+            near = jnp.where((lanes >= base + steps) & (lanes < end), 0.0, parts[q][0])
+            after.append(jnp.concatenate([near, parts[q][1]], axis=1))
+        done_rows = [[spread(parts[group * per + c // 8][w], c % 8) for w in range(2)] for c in range(steps)]
         for q in range((group + 1) * per, tall):
             factors = [lane(q, base + c) for c in range(steps)]
-            parts[q][half] = jnp.where(inside, 0.0, parts[q][half])
-            for w in range(halves):
+            parts[q][0] = jnp.where(inside, 0.0, parts[q][0])
+            for w in range(2):
                 terms = [factors[c] * done_rows[c][w] for c in range(steps)]
                 while len(terms) > 1:
                     terms = [x + y for x, y in zip(terms[::2], terms[1::2])]
@@ -109,16 +107,30 @@
     )
 
 
-def invert(s_ref, blocks):
-    n = s_ref.shape[0]
-    all_lanes = lax.broadcasted_iota(jnp.int32, (n, n), 1)
-    for block in blocks:
-        low = block * NB
-        before, after = eliminate(s_ref[low : low + NB, :], low, 16)
-        update = stacked(before, after)
-        inside = (all_lanes >= low) & (all_lanes < low + NB)
-        s_ref[...] = jnp.where(inside, 0.0, s_ref[...]) - update
-        s_ref[low : low + NB, :] = after - update[low : low + NB, :]
+def invert(s_ref, between=None):
+    lanes = lax.broadcasted_iota(jnp.int32, (128, 128), 1)
+
+    def half(h, carry):
+        if between is not None:
+            pl.when(h == 1)(between)
+        spans = [pl.ds(pl.multiple_of(at * 128, 128), 128) for at in (h, 1 - h)]
+        processed = jnp.full((8, 128), h, jnp.int32) == 1
+        for first in range(0, 128, NB):
+            block = pl.ds(pl.multiple_of(h * 128 + first, NB), NB)
+            before, after = eliminate(s_ref[block, spans[0]], s_ref[block, spans[1]], first, processed, 16)
+            update = stacked(before, after)
+            inside = (lanes >= first) & (lanes < first + NB)
+            for down in range(2):
+                for along in range(2):
+                    kept = s_ref[spans[down], spans[along]]
+                    kept = jnp.where(inside, 0.0, kept) if along == 0 else kept
+                    s_ref[spans[down], spans[along]] = kept - update[128 * down : 128 * down + 128, 128 * along : 128 * along + 128]
+            found = after - update[first : first + NB, :]
+            for along in range(2):
+                s_ref[block, spans[along]] = found[:, 128 * along : 128 * along + 128]
+        return carry
+
+    lax.fori_loop(0, 2, half, 0)
 
 
 def kernel(
@@ -141,7 +153,6 @@
     g_at = ja * n_ka + ka
     h_at = ia * n_ka + ka
     g_tall = rank // n_g
-    n_blocks = rank // NB
 
     def device(z, j, k):
         return {"ia": z, "ja": j, "ka": k}
@@ -274,8 +285,10 @@
     b_whole = b_all[...]
 
     pieces, steps = per // 4, i_dev // per
-
-    for at in range(steps):
+    early = steps * 3 // 4
+
+    def first(step, carry):
+        at = lax.rem(g_at // pieces + 1 + step, steps)
         span = pl.ds(at * per, per)
         left_hi = thi[span].reshape(per * j_dev, k_dev)
         left_lo = tlo[span].reshape(per * j_dev, k_dev)
@@ -284,9 +297,15 @@
         )
         inner = inner.reshape(per, j_dev, rank)
         p_ref[span] = inner
-        a_parts[pl.ds(at * pieces, pieces)] = jnp.sum(inner * b_whole[None], axis=1).reshape(pieces, 4, rank)
-    send(5, n_g, plane, lambda at: a_parts.at[at], lambda at: a_in.at[g_at])
-    a_in[g_at] = a_parts[g_at]
+        summed = jnp.sum(inner * b_whole[None], axis=1)
+        a_parts[pl.ds(at * pieces, pieces)] = summed.reshape(pieces, 4, rank)
+        for e in range(pieces):
+            to = at * pieces + e
+
+            @pl.when(to != g_at)
+            def _():
+                start(5, a_parts.at[to], a_in.at[g_at], device(ia, to // n_ka, lax.rem(to, n_ka)))
+        return carry
 
     def gather_gram(phase, slot, rows):
         g_send[slot] = rows
@@ -294,12 +313,15 @@
         for offset, other in [((0, 0, 0), 1)] + [(offset, other) for offset in ACROSS + NEAR[::-1] for other in (0, 1)]:
             start(phase, g_send.at[slot], rows_of(g_all.at[slot], piece_at), chip(offset, other))
 
+    lax.fori_loop(0, early, first, 0)
     gb_in[ja] = rows_of(gb_mine, piece_at)[...]
     gc_in[ka] = rows_of(gc_mine, piece_at)[...]
     done(3, gb_in.at[pl.ds(0, n_ja - 1)], recv_sem)
     done(4, gc_in.at[pl.ds(0, n_ka - 1)], recv_sem)
     gc_rows[...] = jnp.sum(gc_in[...], axis=0)
     gather_gram(6, 0, jnp.sum(gb_in[...], axis=0) * gc_rows[...])
+    lax.fori_loop(early, steps, first, 0)
+    a_in[g_at] = a_parts[g_at]
 
     done(5, a_in.at[pl.ds(0, n_g - 1)], recv_sem)
     own = jnp.sum(a_in[...], axis=0)
@@ -307,7 +329,7 @@
     a_in2[g_at] = own
     send(7, n_g, plane, lambda at: a_own, lambda at: a_in2.at[g_at])
     done(6, g_all.at[0, pl.ds(0, rank - g_tall)], recv_sem)
-    invert(g_all.at[0], range(n_blocks))
+    invert(g_all.at[0])
     done(7, a_in2.at[pl.ds(0, n_g - 1)], recv_sem)
     for g in range(n_g):
         a_slice[4 * g : 4 * g + 4, :] = a_in2[g]
@@ -339,7 +361,7 @@
         a_mine[g] = a_slice[4 * g : 4 * g + 4, :]
     a_out[0] = a_mine[g_at]
     done(10, g_all.at[1, pl.ds(0, rank - g_tall)], recv_sem)
-    invert(g_all.at[1], range(n_blocks))
+    invert(g_all.at[1])
     done(11, b_in2.at[pl.ds(0, n_h - 1)], recv_sem)
     for h in range(n_h):
         b_slice[4 * h : 4 * h + 4, :] = b_in2[h]
@@ -352,18 +374,22 @@
     for h in range(n_h):
         b_mine[h] = b_slice[4 * h : 4 * h + 4, :]
     b_out[0] = b_mine[h_at]
-    for at in range(steps):
-        span = pl.ds(at * per, per)
-        weights = (a_slice[span, :][:, None, :] * b_now[None]).reshape(per * j_dev, rank)
+    cm_mine[...] = jnp.zeros_like(cm_mine)
+
+    def third(step, carry):
+        span = pl.ds(step * per, per)
+        weights = (a_slice[pl.ds(pl.multiple_of(step * per, per), per), :][:, None, :] * b_now[None]).reshape(per * j_dev, rank)
         whi, wlo = split2(weights)
         left_hi = thi[span].reshape(per * j_dev, k_dev)
         left_lo = tlo[span].reshape(per * j_dev, k_dev)
-        product = dot_bf16(left_hi, whi, ((0,), (0,))) + (
+        cm_mine[...] += dot_bf16(left_hi, whi, ((0,), (0,))) + (
             dot_bf16(left_hi, wlo, ((0,), (0,))) + dot_bf16(left_lo, whi, ((0,), (0,)))
         )
-        cm_mine[...] = product if at == 0 else cm_mine[...] + product
+        return carry
+    lax.fori_loop(0, early, third, 0)
     done(12, gb2_in.at[pl.ds(0, n_ja - 1)], recv_sem)
     gather_gram(14, 2, jnp.sum(gb2_in[...], axis=0) * ga_rows[...])
+    lax.fori_loop(early, steps, third, 0)
     for z in range(n_ia):
         for j in range(n_ja):
             low = 2 * (z * n_ja + j)
@@ -371,12 +397,13 @@
     send(13, n_ja, row, lambda at: cm_parts.at[at], lambda at: cm_in.at[ja])
     cm_in[ja] = cm_parts[ja]
     done(14, g_all.at[2, pl.ds(0, rank - g_tall)], recv_sem)
-    invert(g_all.at[2], range(n_blocks // 2))
-    done(13, cm_in.at[pl.ds(0, n_ja - 1)], recv_sem)
-    cm_sum[...] = jnp.sum(cm_in[...], axis=0)
-    send(15, n_ia, column, lambda at: cm_sum.at[at], lambda at: cm_in2.at[ia])
-    cm_in2[ia] = cm_sum[ia]
-    invert(g_all.at[2], range(n_blocks // 2, n_blocks))
+    def pass_third_products_on():
+        done(13, cm_in.at[pl.ds(0, n_ja - 1)], recv_sem)
+        cm_sum[...] = jnp.sum(cm_in[...], axis=0)
+        send(15, n_ia, column, lambda at: cm_sum.at[at], lambda at: cm_in2.at[ia])
+        cm_in2[ia] = cm_sum[ia]
+
+    invert(g_all.at[2], pass_third_products_on)
     done(15, cm_in2.at[pl.ds(0, n_ia - 1)], recv_sem)
     c_out[0] = dot_f32(jnp.sum(cm_in2[...], axis=0), g_all[2], ((1,), (0,)))
 

time: 83.6 us -> 75.7 us (0.906)
  Pallas kernels: 82.7 us -> 74.8 us
    pallas_call x1, Pallas kernels: 81.3 us -> 73.4 us  [on_device(): pl.pallas_call(functools.partial(kernel, n_ia, n_ja, n_ka), out_shape=out...]
where the time goes in v7:
time: 75.7 us; the launch traced here: 75.6 us
  Pallas kernels  74.8 us (99%)
  between operations  0.8 us (1%)
    pallas_call x1, Pallas kernels, on_device(): pl.pallas_call(functools.partial(kernel, n_ia, n_ja, n_ka), out_shape=out...  73.4 us

profile of v7, /device:TPU:1, one launch (start us, length us, event | category | flops | bytes accessed | tf_op | source)
XLA Modules:
  0.0 75.6 jit_solution(2482243369711343364)
XLA Ops:
  0.6 73.4 %shard_map.58 = (f32[1,4,256]{2,1,0:T(4,128)}, f32[1,4,256]{2,1,0:T(4,128)}, f32[1,2,256]{2,1,0:T(2,128)}) custom-call(f32[128,64,256]{2,1,0:T(8,128)} %t_hbm.1, f32[1,4,256]{2,1,0:T(4,128)} %b_ref.1, f32[1,2,256]{2,1,0:T(2,128)} %c_ref.1), custom_call_target="tpu_custom_call" | custom-call | tf_op jit(solution)/shard_map/pallas_call | solution.py:446
  74.0 1.4 %shard_map.59 = (f32[1,4,256]{2,1,0:T(4,128)}, f32[1,4,256]{2,1,0:T(4,128)}, f32[1,2,256]{2,1,0:T(2,128)}) custom-call(f32[1,4,256]{2,1,0:T(4,128)} %get-tuple-element.6.a_ref, f32[1,4,256]{2,1,0:T(4,128)} %get-tuple-element.7.b_ref, f32[1,2,256]{2,1,0:T(2,128)} %get-tuple-element.8.c_ref), custom_call_target="tpu_custom_call" | custom-call | tf_op jit(solution)/shard_map/pallas_call | solution.py:467

commit v8 on v6

--- a/solution.py
+++ b/solution.py
@@ -274,8 +274,10 @@
     b_whole = b_all[...]
 
     pieces, steps = per // 4, i_dev // per
-
-    for at in range(steps):
+    early = steps * 3 // 4
+
+    def first(step, carry):
+        at = lax.rem(g_at // pieces + 1 + step, steps)
         span = pl.ds(at * per, per)
         left_hi = thi[span].reshape(per * j_dev, k_dev)
         left_lo = tlo[span].reshape(per * j_dev, k_dev)
@@ -284,30 +286,40 @@
         )
         inner = inner.reshape(per, j_dev, rank)
         p_ref[span] = inner
-        a_parts[pl.ds(at * pieces, pieces)] = jnp.sum(inner * b_whole[None], axis=1).reshape(pieces, 4, rank)
-    send(5, n_g, plane, lambda at: a_parts.at[at], lambda at: a_in.at[g_at])
-    a_in[g_at] = a_parts[g_at]
+        summed = jnp.sum(inner * b_whole[None], axis=1)
+        a_parts[pl.ds(at * pieces, pieces)] = summed.reshape(pieces, 4, rank)
+        for e in range(pieces):
+            to = at * pieces + e
+
+            @pl.when(to != g_at)
+            def _():
+                start(5, a_parts.at[to], a_in.at[g_at], device(ia, to // n_ka, lax.rem(to, n_ka)))
+        return carry
 
     def gather_gram(phase, slot, rows):
         g_send[slot] = rows
         rows_of(g_all.at[slot], piece_at)[...] = rows
-        for offset, other in [((0, 0, 0), 1)] + [(offset, other) for offset in ACROSS + NEAR[::-1] for other in (0, 1)]:
+        for offset, other in [(offset, other) for offset in ACROSS[::-1] + NEAR[::-1] for other in (0, 1)] + [((0, 0, 0), 1)]:
             start(phase, g_send.at[slot], rows_of(g_all.at[slot], piece_at), chip(offset, other))
 
+    lax.fori_loop(0, early, first, 0)
     gb_in[ja] = rows_of(gb_mine, piece_at)[...]
     gc_in[ka] = rows_of(gc_mine, piece_at)[...]
     done(3, gb_in.at[pl.ds(0, n_ja - 1)], recv_sem)
     done(4, gc_in.at[pl.ds(0, n_ka - 1)], recv_sem)
     gc_rows[...] = jnp.sum(gc_in[...], axis=0)
     gather_gram(6, 0, jnp.sum(gb_in[...], axis=0) * gc_rows[...])
-
+    lax.fori_loop(early, steps, first, 0)
+    a_in[g_at] = a_parts[g_at]
+
+    done(6, g_all.at[0, pl.ds(0, rank - g_tall)], recv_sem)
+    invert(g_all.at[0], range(3))
     done(5, a_in.at[pl.ds(0, n_g - 1)], recv_sem)
     own = jnp.sum(a_in[...], axis=0)
     a_own[...] = own
     a_in2[g_at] = own
     send(7, n_g, plane, lambda at: a_own, lambda at: a_in2.at[g_at])
-    done(6, g_all.at[0, pl.ds(0, rank - g_tall)], recv_sem)
-    invert(g_all.at[0], range(n_blocks))
+    invert(g_all.at[0], range(3, n_blocks))
     done(7, a_in2.at[pl.ds(0, n_g - 1)], recv_sem)
     for g in range(n_g):
         a_slice[4 * g : 4 * g + 4, :] = a_in2[g]
@@ -352,18 +364,22 @@
     for h in range(n_h):
         b_mine[h] = b_slice[4 * h : 4 * h + 4, :]
     b_out[0] = b_mine[h_at]
-    for at in range(steps):
-        span = pl.ds(at * per, per)
-        weights = (a_slice[span, :][:, None, :] * b_now[None]).reshape(per * j_dev, rank)
+    cm_mine[...] = jnp.zeros_like(cm_mine)
+
+    def third(step, carry):
+        span = pl.ds(step * per, per)
+        weights = (a_slice[pl.ds(pl.multiple_of(step * per, per), per), :][:, None, :] * b_now[None]).reshape(per * j_dev, rank)
         whi, wlo = split2(weights)
         left_hi = thi[span].reshape(per * j_dev, k_dev)
         left_lo = tlo[span].reshape(per * j_dev, k_dev)
-        product = dot_bf16(left_hi, whi, ((0,), (0,))) + (
+        cm_mine[...] += dot_bf16(left_hi, whi, ((0,), (0,))) + (
             dot_bf16(left_hi, wlo, ((0,), (0,))) + dot_bf16(left_lo, whi, ((0,), (0,)))
         )
-        cm_mine[...] = product if at == 0 else cm_mine[...] + product
+        return carry
+    lax.fori_loop(0, early, third, 0)
     done(12, gb2_in.at[pl.ds(0, n_ja - 1)], recv_sem)
     gather_gram(14, 2, jnp.sum(gb2_in[...], axis=0) * ga_rows[...])
+    lax.fori_loop(early, steps, third, 0)
     for z in range(n_ia):
         for j in range(n_ja):
             low = 2 * (z * n_ja + j)

time: 83.6 us -> 74.9 us (0.90)
  Pallas kernels: 82.7 us -> 73.9 us
    pallas_call x1, Pallas kernels: 81.3 us -> 72.5 us  [on_device(): pl.pallas_call(functools.partial(kernel, n_ia, n_ja, n_ka), out_shape=out...]
where the time goes in v8:
time: 74.9 us; the launch traced here: 74.7 us
  Pallas kernels  73.9 us (99%)
  between operations  0.82 us (1%)
    pallas_call x1, Pallas kernels, on_device(): pl.pallas_call(functools.partial(kernel, n_ia, n_ja, n_ka), out_shape=out...  72.5 us

profile of v8, /device:TPU:1, one launch (start us, length us, event | category | flops | bytes accessed | tf_op | source)
XLA Modules:
  0.0 74.7 jit_solution(12135990526460145901)
XLA Ops:
  0.6 72.5 %shard_map.58 = (f32[1,4,256]{2,1,0:T(4,128)}, f32[1,4,256]{2,1,0:T(4,128)}, f32[1,2,256]{2,1,0:T(2,128)}) custom-call(f32[128,64,256]{2,1,0:T(8,128)} %t_hbm.1, f32[1,4,256]{2,1,0:T(4,128)} %b_ref.1, f32[1,2,256]{2,1,0:T(2,128)} %c_ref.1), custom_call_target="tpu_custom_call" | custom-call | tf_op jit(solution)/shard_map/pallas_call | solution.py:435
  73.1 1.4 %shard_map.59 = (f32[1,4,256]{2,1,0:T(4,128)}, f32[1,4,256]{2,1,0:T(4,128)}, f32[1,2,256]{2,1,0:T(2,128)}) custom-call(f32[1,4,256]{2,1,0:T(4,128)} %get-tuple-element.6.a_ref, f32[1,4,256]{2,1,0:T(4,128)} %get-tuple-element.7.b_ref, f32[1,2,256]{2,1,0:T(2,128)} %get-tuple-element.8.c_ref), custom_call_target="tpu_custom_call" | custom-call | tf_op jit(solution)/shard_map/pallas_call | solution.py:456

commit v9 on v8

--- a/solution.py
+++ b/solution.py
@@ -313,13 +313,13 @@
     a_in[g_at] = a_parts[g_at]
 
     done(6, g_all.at[0, pl.ds(0, rank - g_tall)], recv_sem)
-    invert(g_all.at[0], range(3))
+    invert(g_all.at[0], range(2))
     done(5, a_in.at[pl.ds(0, n_g - 1)], recv_sem)
     own = jnp.sum(a_in[...], axis=0)
     a_own[...] = own
     a_in2[g_at] = own
     send(7, n_g, plane, lambda at: a_own, lambda at: a_in2.at[g_at])
-    invert(g_all.at[0], range(3, n_blocks))
+    invert(g_all.at[0], range(2, n_blocks))
     done(7, a_in2.at[pl.ds(0, n_g - 1)], recv_sem)
     for g in range(n_g):
         a_slice[4 * g : 4 * g + 4, :] = a_in2[g]

time: 74.9 us -> 74.7 us (level)
  no operation moved by 1% of the time
where the time goes in v9:
time: 74.7 us; the launch traced here: 74.5 us
  Pallas kernels  73.7 us (99%)
  between operations  0.82 us (1%)
    pallas_call x1, Pallas kernels, on_device(): pl.pallas_call(functools.partial(kernel, n_ia, n_ja, n_ka), out_shape=out...  72.3 us

profile of v9, /device:TPU:1, one launch (start us, length us, event | category | flops | bytes accessed | tf_op | source)
XLA Modules:
  0.0 74.5 jit_solution(16041200432492775032)
XLA Ops:
  0.6 72.3 %shard_map.58 = (f32[1,4,256]{2,1,0:T(4,128)}, f32[1,4,256]{2,1,0:T(4,128)}, f32[1,2,256]{2,1,0:T(2,128)}) custom-call(f32[128,64,256]{2,1,0:T(8,128)} %t_hbm.1, f32[1,4,256]{2,1,0:T(4,128)} %b_ref.1, f32[1,2,256]{2,1,0:T(2,128)} %c_ref.1), custom_call_target="tpu_custom_call" | custom-call | tf_op jit(solution)/shard_map/pallas_call | solution.py:435
  72.9 1.4 %shard_map.59 = (f32[1,4,256]{2,1,0:T(4,128)}, f32[1,4,256]{2,1,0:T(4,128)}, f32[1,2,256]{2,1,0:T(2,128)}) custom-call(f32[1,4,256]{2,1,0:T(4,128)} %get-tuple-element.6.a_ref, f32[1,4,256]{2,1,0:T(4,128)} %get-tuple-element.7.b_ref, f32[1,2,256]{2,1,0:T(2,128)} %get-tuple-element.8.c_ref), custom_call_target="tpu_custom_call" | custom-call | tf_op jit(solution)/shard_map/pallas_call | solution.py:456
